TPU v7x, 256 devices: a whole 4x4x8 slice. The times are simulated.
256 devices in a mesh: lon: 16 (over x_hi, z), tp: 16 (over y, x_lo, core).
Axes of the slice: x: 4 (x_hi: 2, x_lo: 2; x = x_hi * 2 + x_lo), y: 4, z: 8, core: 2. Of those that a mesh axis runs over, the one named last changes fastest.
Arguments:
- activations: bfloat16 [384, 2, 12, 1024], P('lon'), may hold values from -6 to 6
- qkv_weight: bfloat16 [3, 1024, 1024], P(None, None, 'tp'), may hold values from -0.1875 to 0.1875
- proj_weight: bfloat16 [1024, 1024], P('tp'), may hold values from -0.1875 to 0.1875
- pos_bias: float32 [16, 144, 144], P('tp'), may hold values from -3 to 302
- out_grad: bfloat16 [384, 2, 12, 1024], P('lon', None, None, 'tp'), may hold values from -6 to 6
Outputs:
- in_grad: bfloat16 [384, 2, 12, 1024], P('lon', None, None, 'tp')
- qkv_grad: float32 [3, 1024, 1024], P(None, 'lon', 'tp')
- proj_grad: float32 [1024, 1024], P('tp', 'lon')
- bias_grad: float32 [16, 144, 144], P('tp', 'lon')
All inputs are finite; a program needn't handle non-finite values.
Results may differ from a plain program's by a relative error of at most 0.019.
Values may be sent and summed in bfloat16 or wider, within the bound.
A program may use at most 384 MiB of HBM per device.

v0:
```python
import jax
import jax.numpy as jnp
from jax import lax
from jax.sharding import PartitionSpec as P

WIN_LON = 12
HD = 64


def shifted_2(x, axis, by):
    length = lax.axis_size(axis)
    return lax.ppermute(x, axis, [(i, (i + by) % length) for i in range(length)])


def to_windows(field):
    lon_len, rows, cells, width = field.shape
    count = lon_len // WIN_LON
    grouped = field.reshape(count, WIN_LON, rows, cells, width).transpose(0, 2, 1, 3, 4)
    return grouped.reshape(count * rows, WIN_LON * cells, width)


def from_windows(field, lon_len, rows, cells):
    count = lon_len // WIN_LON
    width = field.shape[-1]
    grouped = field.reshape(count, rows, WIN_LON, cells, width).transpose(0, 2, 1, 3, 4)
    return grouped.reshape(lon_len, rows, cells, width)


def per_device(activations, qkv_weight, proj_weight, pos_bias, out_grad):
    half_win = WIN_LON // 2
    att_scale = 1.0 / jnp.sqrt(jnp.float32(HD))
    lon_len, rows, cells, width = activations.shape
    share = out_grad.shape[3]
    heads_here = pos_bias.shape[0]
    head_local = qkv_weight.shape[2]
    head_size = head_local // heads_here
    tokens_win = WIN_LON * cells
    widened = activations.astype(jnp.float32)
    centered = widened - jnp.mean(widened, axis=-1, keepdims=True)
    inv_dev = lax.rsqrt(jnp.mean(centered * centered, axis=-1, keepdims=True) + 1e-05)
    normed = centered * inv_dev
    normed_low = normed.astype(jnp.bfloat16)
    lead_tokens, lead_grads = shifted_2((normed_low[:half_win], out_grad[:half_win]), "lon", -1)
    shifted = jnp.concatenate([normed_low[half_win:], lead_tokens], axis=0)
    grad_local = jnp.concatenate([out_grad[half_win:], lead_grads], axis=0)
    grad_shift = lax.all_gather(grad_local, "tp", axis=3, tiled=True)
    windows = to_windows(shifted)
    grad_win = to_windows(grad_shift)
    num_windows = windows.shape[0]
    qkv_all = jnp.einsum(
        "ntd,cde->cnte", windows, qkv_weight, preferred_element_type=jnp.float32
    ).astype(jnp.bfloat16)
    query = qkv_all[0].reshape(num_windows, tokens_win, heads_here, head_size)
    key_part = qkv_all[1].reshape(num_windows, tokens_win, heads_here, head_size)
    value_part = qkv_all[2].reshape(num_windows, tokens_win, heads_here, head_size)
    scores = (
        jnp.einsum("nqhe,nkhe->nhqk", query, key_part, preferred_element_type=jnp.float32)
        * att_scale
        + pos_bias[None]
    )
    probs = jax.nn.softmax(scores, axis=-1)
    probs_low = probs.astype(jnp.bfloat16)
    attended = jnp.einsum(
        "nhqk,nkhe->nqhe", probs_low, value_part, preferred_element_type=jnp.float32
    ).astype(jnp.bfloat16)
    attended = attended.reshape(num_windows, tokens_win, head_local)
    grad_attn = jnp.einsum(
        "ntd,ed->nte", grad_win, proj_weight, preferred_element_type=jnp.float32
    ).astype(jnp.bfloat16)
    grad_heads = grad_attn.reshape(num_windows, tokens_win, heads_here, head_size)
    grad_probs = jnp.einsum(
        "nqhe,nkhe->nhqk", grad_heads, value_part, preferred_element_type=jnp.float32
    )
    grad_scores = probs * (grad_probs - jnp.sum(grad_probs * probs, axis=-1, keepdims=True))
    grad_value = jnp.einsum(
        "nhqk,nqhe->nkhe", probs_low, grad_heads, preferred_element_type=jnp.float32
    ).astype(jnp.bfloat16)
    grad_low = grad_scores.astype(jnp.bfloat16)
    grad_query = (
        jnp.einsum("nhqk,nkhe->nqhe", grad_low, key_part, preferred_element_type=jnp.float32)
        * att_scale
    ).astype(jnp.bfloat16)
    grad_key = (
        jnp.einsum("nhqk,nqhe->nkhe", grad_low, query, preferred_element_type=jnp.float32)
        * att_scale
    ).astype(jnp.bfloat16)
    grad_qkv = jnp.stack([grad_query, grad_key, grad_value]).reshape(
        3, num_windows, tokens_win, head_local
    )
    proj_part = jnp.einsum("nte,ntd->ed", attended, grad_win, preferred_element_type=jnp.float32)
    qkv_part = jnp.einsum("ntd,cnte->cde", windows, grad_qkv, preferred_element_type=jnp.float32)
    bias_part = jnp.sum(grad_scores, axis=0)
    proj_grad, qkv_grad, bias_grad = (
        lax.psum_scatter(
            proj_part.astype(jnp.bfloat16), "lon", scatter_dimension=1, tiled=True
        ).astype(jnp.float32),
        lax.psum_scatter(
            qkv_part.astype(jnp.bfloat16), "lon", scatter_dimension=1, tiled=True
        ).astype(jnp.float32),
        lax.psum_scatter(
            bias_part.astype(jnp.bfloat16), "lon", scatter_dimension=1, tiled=True
        ).astype(jnp.float32),
    )
    grad_windows = jnp.einsum(
        "cnte,cde->ntd", grad_qkv, qkv_weight, preferred_element_type=jnp.float32
    )
    grad_hidden = from_windows(grad_windows, lon_len, rows, cells)
    cut_point = lon_len - half_win
    moved = shifted_2(grad_hidden[cut_point:].astype(jnp.bfloat16), "lon", 1).astype(jnp.float32)
    pending = jnp.concatenate([moved, grad_hidden[:cut_point]], axis=0)
    summed = lax.psum(pending.astype(jnp.bfloat16), "tp").astype(jnp.float32)
    offset = lax.axis_index("tp") * share
    normed_share = lax.dynamic_slice_in_dim(normed, offset, share, 3)
    first = jnp.mean(summed, axis=-1, keepdims=True)
    second = jnp.mean(summed * normed, axis=-1, keepdims=True)
    grad_share = lax.dynamic_slice_in_dim(summed, offset, share, 3)
    in_grad = (
        out_grad.astype(jnp.float32) + inv_dev * (grad_share - first - normed_share * second)
    ).astype(jnp.bfloat16)
    return (in_grad, qkv_grad, proj_grad, bias_grad)


def solution(mesh):
    placed = (
        P("lon", None, None, None),
        P(None, None, "tp"),
        P("tp", None),
        P("tp", None, None),
        P("lon", None, None, "tp"),
    )
    return jax.shard_map(
        per_device,
        mesh=mesh,
        in_specs=placed,
        out_specs=(
            P("lon", None, None, "tp"),
            P(None, "lon", "tp"),
            P("tp", "lon"),
            P("tp", "lon", None),
        ),
        check_vma=False,
    )
```

profile of v0, /device:TPU:1, one launch (start us, length us, event | category | flops | bytes accessed | tf_op | source)
XLA Modules:
  0.0 630.0 jit_solution(13336877084051343753)
XLA Ops:
  8.1 8.9 %collective-permute-start.1 = (bf16[6,2,12,64]{3,0,2,1:T(8,128)(2,1)S(1)}, bf16[6,2,12,64]{3,0,2,1:T(8,128)(2,1)S(1)}, u32[]{:S(2)}, u32[]{:S(2)}) collective-permute-start(bf16[6,2,12,64]{3,0,2,1:T(8,128)(2,1)S(1)} %copy.107), channel_id=1, source_target_pairs={{0,240},{16,0},{32,16},{48,32},{64,48},{80,64},{96,80},{112,96},{1... | collective-permute-start | bytes 55304 | tf_op jit(solution)/shard_map/ppermute | solution.py:12
  17.0 2.3 convert_reduce_fusion
  20.7 1.7 fusion.3
  24.0 4.4 collective-permute-start
  29.1 1.7 copy.72
  30.8 2.1 collective-permute-done
  36.7 2.0 fusion.10
  40.0 24.9 %all-gather.2.cloned.1.call-done = bf16[24,2,12,1024]{0,1,2,3:T(2,128)(2,1)} async-done(((bf16[24,2,12,64]{0,1,2,3:T(2,128)(2,1)}), bf16[24,2,12,1024]{0,1,2,3:T(2,128)(2,1)}) %all-gather.2.cloned.1.call-update) | async-done | bytes 1179664 | tf_op jit(solution)/shard_map/all_gather | solution.py:46
  64.8 15.6 %copy.76 = bf16[24,2,12,1024]{3,1,2,0:T(2,128)(2,1)} copy(bf16[24,2,12,1024]{0,1,2,3:T(2,128)(2,1)} %all-gather.2.cloned.1.call-done) | data formatting | bytes 2359296 | tf_op jit(solution)/shard_map/all_gather | solution.py:46
  83.1 1.9 convolution_convert_fusion.3
  85.0 2.3 fusion.14
  87.3 2.0 fusion.17
  90.2 1.8 copy.102
  92.0 2.6 fusion.9
  94.6 1.6 copy.100
  100.1 1.6 collective-permute-start.2
  102.4 11.9 %collective-permute-done.2 = bf16[6,2,12,1024]{3,1,2,0:T(2,128)(2,1)S(1)} collective-permute-done((bf16[6,2,12,1024]{3,1,2,0:T(2,128)(2,1)S(1)}, bf16[6,2,12,1024]{3,1,2,0:T(2,128)(2,1)S(1)}, u32[]{:S(2)}, u32[]{:S(2)}) %collective-permute-start.2) | collective-permute-done | bytes 294944 | tf_op jit(solution)/shard_map/ppermute | solution.py:12
  114.3 2.6 pad_maximum_fusion.1
  118.9 60.9 %all-reduce = bf16[1,144,144]{2,0,1:T(2,128)(2,1)S(1)} all-reduce(bf16[1,144,144]{2,0,1:T(2,128)(2,1)S(1)} %copy.88), channel_id=4, replica_groups=mesh['lon'=16,'tp'=16] {'lon'}, use_global_device_ids=true, to_apply=%region_11.0.clone | all-reduce | flops 20736 | bytes 82944
  180.5 103.6 %reduce-scatter.9.cloned.1.call-done = bf16[64,64]{1,0:T(8,128)(2,1)} async-done(((bf16[1024,64]{1,0:T(8,128)(2,1)}), bf16[64,64]{1,0:T(8,128)(2,1)}) %reduce-scatter.9.cloned.1.call-update) | async-done | bytes 8208
  285.5 198.2 %reduce-scatter.7.cloned.1.call-done = bf16[64,192]{1,0:T(8,128)(2,1)} async-done(((bf16[1024,192]{1,0:T(8,128)(2,1)}), bf16[64,192]{1,0:T(8,128)(2,1)}) %reduce-scatter.7.cloned.1.call-update) | async-done | bytes 24592
  485.4 129.3 %all-reduce.3.cloned.1.call-done = bf16[24,2,12,1024]{3,1,2,0:T(2,128)(2,1)} async-done(((bf16[24,2,12,1024]{3,1,2,0:T(2,128)(2,1)}), bf16[24,2,12,1024]{3,1,2,0:T(2,128)(2,1)}) %all-reduce.3.cloned.1.call-update) | async-done | bytes 1179664 | tf_op jit(solution)/shard_map/psum | solution.py:111
  614.7 5.2 convert_reduce_fusion.1
  621.0 2.4 add_convert_fusion
  (72 shorter events, 23.9 us)
Async XLA Ops:
  7.2 29.6 %copy-start = (bf16[3,1024,64]{1,2,0:T(8,128)(2,1)S(1)}, bf16[3,1024,64]{1,2,0:T(8,128)(2,1)}, u32[]{:S(2)}) copy-start(bf16[3,1024,64]{1,2,0:T(8,128)(2,1)} %param.6) | copy-start | bytes 1179652
  7.2 12.1 %slice-start = ((bf16[24,2,12,64]{3,1,2,0:T(2,128)(2,1)}), bf16[18,2,12,64]{3,1,2,0:T(2,128)(2,1)S(1)}, s32[]{:S(2)}) async-start(bf16[24,2,12,64]{3,1,2,0:T(2,128)(2,1)} %param.9), calls=%async_computation.6 | async-start | bytes 221184 | tf_op jit(solution)/shard_map/slice | solution.py:45
  7.2 57.6 %all-gather.2.cloned.1.call-start = ((), (), s32[]{:S(2)}) async-start(), calls=%async_computation.2 | async-start | bytes 6684672 | tf_op jit(solution)/shard_map/all_gather | solution.py:46
  8.1 11.3 %collective-permute-start.1 = (bf16[6,2,12,64]{3,0,2,1:T(8,128)(2,1)S(1)}, bf16[6,2,12,64]{3,0,2,1:T(8,128)(2,1)S(1)}, u32[]{:S(2)}, u32[]{:S(2)}) collective-permute-start(bf16[6,2,12,64]{3,0,2,1:T(8,128)(2,1)S(1)} %copy.107), channel_id=1, source_target_pairs={{0,240},{16,0},{32,16},{48,32},{64,48},{80,64},{96,80},{112,96},{1... | collective-permute-start | bytes 55304 | tf_op jit(solution)/shard_map/ppermute | solution.py:12
  19.3 1.3 copy-start.1
  20.5 263.6 %reduce-scatter.9.cloned.1.call-start = ((), (), s32[]{:S(2)}) async-start(), calls=%async_computation.5 | async-start | bytes 278528
  24.0 8.9 %collective-permute-start = (bf16[6,2,12,1024]{3,1,2,0:T(2,128)(2,1)S(1)}, bf16[6,2,12,1024]{3,1,2,0:T(2,128)(2,1)S(1)}, u32[]{:S(2)}, u32[]{:S(2)}) collective-permute-start(bf16[6,2,12,1024]{3,1,2,0:T(2,128)(2,1)S(1)} %slice.39), channel_id=1, source_target_pairs={{0,240},{16,0},{32,16},{48,32},{64,48},{80,64},{96,80},{112,96},{1... | collective-permute-start | bytes 884744 | tf_op jit(solution)/shard_map/ppermute | solution.py:12
  36.7 2.0 copy-start.9
  38.7 41.7 %copy-start.7 = (bf16[3,4,144,64]{2,3,0,1:T(8,128)(2,1)}, bf16[3,4,144,64]{2,3,0,1:T(8,128)(2,1)S(1)}, u32[]{:S(2)}) copy-start(bf16[3,4,144,64]{2,3,0,1:T(8,128)(2,1)S(1)} %fusion.10) | copy-start | bytes 663556
  83.1 1.9 copy-start.3
  87.3 2.0 copy-start.5
  87.3 2.0 copy-start.8
  89.8 2.2 copy-start.4
  92.0 391.8 %reduce-scatter.7.cloned.1.call-start = ((), (), s32[]{:S(2)}) async-start(), calls=%async_computation.4 | async-start | bytes 557056
  96.2 1.4 copy-start.10
  97.6 517.1 %all-reduce.3.cloned.1.call-start = ((), (), s32[]{:S(2)}) async-start(), calls=%async_computation.3 | async-start | bytes 2359296 | tf_op jit(solution)/shard_map/psum | solution.py:111
  100.1 14.1 %collective-permute-start.2 = (bf16[6,2,12,1024]{3,1,2,0:T(2,128)(2,1)S(1)}, bf16[6,2,12,1024]{3,1,2,0:T(2,128)(2,1)S(1)}, u32[]{:S(2)}, u32[]{:S(2)}) collective-permute-start(bf16[6,2,12,1024]{3,1,2,0:T(2,128)(2,1)S(1)} %slice.43), channel_id=1, source_target_pairs={{0,16},{16,32},{32,48},{48,64},{64,80},{80,96},{96,112},{112,128},... | collective-permute-start | bytes 884744 | tf_op jit(solution)/shard_map/ppermute | solution.py:12
  116.9 0.7 copy-start.11
  614.7 5.3 copy-start.2
  620.0 1.0 copy-start.6
Sparse Core Ops, SparseCore 0:
  20.6 44.1 all-gather.1
  92.1 191.9 reduce-scatter.8
  288.4 195.3 reduce-scatter.6
  486.2 128.4 all-reduce.2
where the time goes:
time: 631 us; the launch traced here: 630 us
  waiting for transfers between devices  470 us (74%)
  blocking collectives  60.9 us (10%)
  local copies, waits for them, and re-layouts  36.2 us (6%)
  other arithmetic  19.7 us (3%)
  starting transfers between devices  15.1 us (2%)
  between operations  14.8 us (2%)
  matrix products  13.3 us (2%)
    unnamed x6, waiting for transfers between devices  302 us
    psum x1, waiting for transfers between devices, per_device(): summed = lax.psum(pending.astype(jnp.bfloat16), 'tp').astype(jnp.float32)  129 us
    unnamed x1, blocking collectives  60.9 us
    all_gather x1, waiting for transfers between devices, per_device(): grad_shift = lax.all_gather(grad_local, 'tp', axis=3, tiled=True)  24.9 us
    all_gather x1, local copies, waits for them, and re-layouts, per_device(): grad_shift = lax.all_gather(grad_local, 'tp', axis=3, tiled=True)  15.6 us
    ppermute x3, starting transfers between devices, shifted_2(): lax.ppermute(x, axis, [(i, (i + by) % length) for i in range(length)])  14.9 us
    ppermute x3, waiting for transfers between devices, shifted_2(): lax.ppermute(x, axis, [(i, (i + by) % length) for i in range(length)])  14 us
  transfers between devices with their start and end apart: 7, of which 6 were waited for; matrix products, arithmetic and copies ran while one was open for 5% of the time, Pallas kernels for 0%

commit v1 on v0

v1 whole, which is shorter than its diff:
```python
import functools

import jax
import jax.numpy as jnp
from jax import lax
from jax.experimental import pallas as pl
from jax.experimental.pallas import tpu as pltpu
from jax.sharding import PartitionSpec as P

BF = jnp.bfloat16
F32 = jnp.float32
MESH = pl.DeviceIdType.MESH

LON = 24
ROWS = 2
CELLS = 12
D = 1024
HD = 64
WT = 144
NT = 288
HALF = 72
HPAD = 80
CHIPS = 8
ZL = 8
SCALE = 0.125


def nt(a, b):
    return lax.dot_general(a, b, (((1,), (1,)), ((), ())), preferred_element_type=F32)


def tn(a, b):
    return lax.dot_general(a, b, (((0,), (0,)), ((), ())), preferred_element_type=F32)


def nn(a, b):
    return jnp.dot(a, b, preferred_element_type=F32)


def kernel(
    act,
    qw,
    pw,
    pb,
    og,
    out_in,
    out_qkv,
    out_proj,
    out_bias,
    act_v,
    og_v,
    qw_v,
    pw_v,
    pb_v,
    xs,
    hs,
    hsend,
    hrecv,
    nf,
    xb,
    inv_s,
    pf,
    psend,
    precv,
    tsh,
    tsend,
    trecv,
    wsend,
    wrecv,
    pwr,
    pbr,
    w2,
    pw2,
    g,
    qkv_s,
    probs_s,
    att_s,
    dqkv_s,
    m_own,
    m_send,
    m_recv,
    b_own,
    b_send,
    b_recv,
    xsend,
    xrecv,
    bxs,
    bxr,
    zown,
    zsend,
    zrecv,
    rs_send,
    rs_recv,
    fin,
    fsend,
    frecv,
    fhs,
    fhr0,
    fhr1,
    outf,
    lsem,
    ssem,
    rsem,
):
    tp = lax.axis_index("tp")
    lon = lax.axis_index("lon")
    core = lax.rem(tp, 2)
    chip = lax.div(tp, 2)
    xh = lax.div(lon, ZL)
    z = lax.rem(lon, ZL)
    sib_tp = chip * 2 + 1 - core
    up = lax.rem(lon + 1, 16)
    down = lax.rem(lon + 15, 16)
    sib = {"tp": sib_tp}
    down_same = {"lon": down}
    up_same = {"lon": up}
    up_cross = {"lon": up, "tp": sib_tp}
    down_cross = {"lon": down, "tp": sib_tp}
    across = {"lon": (1 - xh) * ZL + z}
    chips = [None] + [{"tp": lax.rem(chip + k, CHIPS) * 2 + core} for k in range(1, CHIPS)]
    zs = [None] + [{"lon": xh * ZL + lax.rem(z + k, ZL)} for k in range(1, ZL)]

    barrier = pltpu.get_barrier_semaphore()
    peers = [sib] + chips[1:] + [down_same, up_same, up_cross, down_cross, across] + zs[1:]
    for peer in peers:
        pl.semaphore_signal(barrier, inc=1, device_id=peer, device_id_type=MESH)

    loads = [
        pltpu.make_async_copy(act.at[:, core], act_v, lsem.at[0]),
        pltpu.make_async_copy(og, og_v, lsem.at[1]),
        pltpu.make_async_copy(qw, qw_v, lsem.at[2]),
        pltpu.make_async_copy(pw, pw_v, lsem.at[3]),
        pltpu.make_async_copy(pb, pb_v, lsem.at[4]),
    ]
    for load in loads:
        load.start()

    count = [0]

    def remote(src, dst, peer):
        i = count[0]
        count[0] += 1
        return pltpu.make_async_remote_copy(
            src_ref=src,
            dst_ref=dst,
            send_sem=ssem.at[i],
            recv_sem=rsem.at[i],
            device_id=peer,
            device_id_type=MESH,
        )

    started = []

    def go(copy):
        copy.start()
        started.append(copy)
        return copy

    low = lax.broadcasted_iota(jnp.int32, (1, 128), 1) < HD

    loads[1].wait()
    for l in range(LON):
        both = jnp.concatenate([og_v[l, 0].astype(F32), og_v[l, 1].astype(F32)], axis=1)
        pf[CELLS * l : CELLS * (l + 1), :] = both
    psend[...] = pf[...].astype(BF)

    loads[0].wait()
    for l in range(LON):
        piece = act_v[l].astype(F32)
        if l < 6:
            hs[CELLS * l : CELLS * (l + 1), :] = piece
        else:
            xs[CELLS * (l - 6) : CELLS * (l - 5), :] = piece
    hs[HALF:HPAD, :] = jnp.zeros((HPAD - HALF, D), F32)
    hsend[...] = hs[...].astype(BF)

    loads[2].wait()
    for i in range(4):
        r = pl.ds(256 * i, 256)
        wsend[r, :] = jnp.concatenate(
            [qw_v[0, r].astype(F32), qw_v[1, r].astype(F32)], axis=1
        ).astype(BF)
    for i in range(2):
        a = pl.ds(256 * i, 256)
        b = pl.ds(512 + 256 * i, 256)
        wsend[pl.ds(1024 + 256 * i, 256), :] = jnp.concatenate(
            [qw_v[2, a].astype(F32), qw_v[2, b].astype(F32)], axis=1
        ).astype(BF)
    loads[3].wait()
    loads[4].wait()

    def norm(w):
        def body(i, carry):
            r = pl.ds(pl.multiple_of(WT * w + 48 * i, 16), 48)
            x = xs[r, :]
            cen = x - jnp.mean(x, axis=1, keepdims=True)
            inv = lax.rsqrt(jnp.mean(cen * cen, axis=1, keepdims=True) + 1e-05)
            y = cen * inv
            nf[r, :] = y
            xb[r, :] = y.astype(BF)
            inv_s[r, :] = jnp.broadcast_to(inv, (48, 128))
            return carry

        lax.fori_loop(0, 3, body, 0)

    norm(0)

    pl.semaphore_wait(barrier, len(peers))

    p_copy = go(remote(psend, precv, sib))
    h_copy = go(remote(hsend, hrecv, down_same))
    w_copy = go(remote(wsend, wrecv, sib))
    pw_copy = go(remote(pw_v, pwr, sib))
    pb_copy = go(remote(pb_v, pbr, sib))

    p_copy.wait_recv()
    mine = low == (core == 0)
    merged = jnp.where(mine, pf[...], pltpu.roll(precv[...].astype(F32), HD, 1))
    tsend[...] = merged[0:HPAD].astype(BF)
    t_copy = go(remote(tsend, trecv, down_same))
    tsh[0 : NT - HALF, :] = merged[HALF:NT]
    g[0, chip] = merged[HALF : HALF + WT].astype(BF)
    ag = [[], []]
    for k in range(1, CHIPS):
        ag[0].append(go(remote(g.at[0, chip], g.at[0, chip], chips[k])))

    w_copy.wait_recv()
    for i in range(4):
        r = pl.ds(256 * i, 256)
        got = wrecv[r, :].astype(F32)
        w2[r, 0:128] = jnp.where(
            low, jnp.concatenate([qw_v[0, r].astype(F32)] * 2, axis=1), pltpu.roll(got, HD, 1)
        ).astype(BF)
        w2[r, 128:256] = jnp.where(
            low, jnp.concatenate([qw_v[1, r].astype(F32)] * 2, axis=1), got
        ).astype(BF)
        got = wrecv[pl.ds(1024 + 256 * (i % 2), 256), :].astype(F32)
        if i < 2:
            got = pltpu.roll(got, HD, 1)
        w2[r, 256:384] = jnp.where(
            low, jnp.concatenate([qw_v[2, r].astype(F32)] * 2, axis=1), got
        ).astype(BF)
    wsum = jnp.sum(w2[...].astype(F32), axis=0, keepdims=True)
    pw_copy.wait_recv()
    pw2[0:HD, :] = pw_v[...]
    pw2[HD:128, :] = pwr[...]
    pb_copy.wait_recv()

    def forward(w):
        r = pl.ds(WT * w, WT)
        qkv = nn(xb[r, :], w2[...]).astype(BF)
        qkv_s[r, :] = qkv
        q2, k2, v2 = qkv[:, 0:128], qkv[:, 128:256], qkv[:, 256:384]
        att = []
        for h in range(2):
            keep = low if h == 0 else jnp.logical_not(low)
            s = nt(jnp.where(keep, q2, jnp.zeros_like(q2)), k2) * SCALE
            s = s + (pb_v[0] if h == 0 else pbr[0])
            e = jnp.exp(s - jnp.max(s, axis=1, keepdims=True))
            p = e * (1.0 / jnp.sum(e, axis=1, keepdims=True))
            probs_s[w, h] = p
            att.append(nn(p.astype(BF), v2))
        att_s[r, :] = jnp.where(low, att[0], att[1]).astype(BF)

    forward(0)

    t_copy.wait_recv()
    tsh[NT - HALF : NT, :] = trecv[...].astype(F32)[0:HALF]
    g[1, chip] = tsh[WT:NT, :].astype(BF)
    for k in range(1, CHIPS):
        ag[1].append(go(remote(g.at[1, chip], g.at[1, chip], chips[k])))

    h_copy.wait_recv()
    xs[NT - HALF : NT, :] = hrecv[...].astype(F32)[0:HALF]
    norm(1)
    forward(1)

    def backward(w):
        r = pl.ds(WT * w, WT)
        grads = jnp.concatenate([g[w, m] for m in range(CHIPS)], axis=1)
        ga = nt(grads, pw2[...]).astype(BF)
        q2, k2, v2 = qkv_s[r, 0:128], qkv_s[r, 128:256], qkv_s[r, 256:384]
        dq, dk, dv = [], [], []
        for h in range(2):
            keep = low if h == 0 else jnp.logical_not(low)
            p = probs_s[w, h]
            gp = nt(jnp.where(keep, ga, jnp.zeros_like(ga)), v2)
            ds = p * (gp - jnp.sum(gp * p, axis=1, keepdims=True))
            if w == 0:
                b_own[h] = ds
            else:
                b_own[h] = b_own[h] + ds
            dl = ds.astype(BF)
            dv.append(tn(p.astype(BF), ga))
            dq.append(nn(dl, k2) * SCALE)
            dk.append(tn(dl, q2) * SCALE)
        dqkv_s[r, 0:128] = jnp.where(low, dq[0], dq[1]).astype(BF)
        dqkv_s[r, 128:256] = jnp.where(low, dk[0], dk[1]).astype(BF)
        dqkv_s[r, 256:384] = jnp.where(low, dv[0], dv[1]).astype(BF)

    rs = [[], []]

    def input_grad(w):
        r = pl.ds(WT * w, WT)
        dq = dqkv_s[r, :]
        wide = dq.astype(F32)
        inv = inv_s[r, 0:1]
        first = jnp.sum(wide * wsum, axis=1, keepdims=True) * (1.0 / D)
        second = jnp.sum(wide * qkv_s[r, :].astype(F32), axis=1, keepdims=True) * (1.0 / D)
        for m in range(CHIPS):
            part = nt(dq, w2[128 * m : 128 * (m + 1), :])
            part = inv * (part - first - nf[r, 128 * m : 128 * (m + 1)] * second)
            rs_send[w, m] = part.astype(BF)
        for k in range(1, CHIPS):
            to = lax.rem(chip + k, CHIPS)
            rs[w].append(go(remote(rs_send.at[w, to], rs_recv.at[w, k - 1], chips[k])))

    for copy in ag[0]:
        copy.wait_recv()
    backward(0)
    input_grad(0)

    for copy in ag[1]:
        copy.wait_recv()
    backward(1)

    b_send[:, 0:WT] = b_own[1].astype(BF)
    b_copy = go(remote(b_send, b_recv, sib))
    grads = [jnp.concatenate([g[w, m] for w in range(2)], axis=0) for m in range(CHIPS)]
    for m in range(CHIPS):
        x = xb[:, 128 * m : 128 * (m + 1)]
        for c in range(4):
            if c < 3:
                part = tn(dqkv_s[:, 128 * c : 128 * (c + 1)], x)
            else:
                part = tn(att_s[...], grads[m])
            m_own[m, HD * c : HD * (c + 1), :] = part[0:HD]
            m_send[m, HD * c : HD * (c + 1), :] = part[HD:128].astype(BF)
    far = (1 - xh) * 4
    near = xh * 4
    m_copies = [
        go(remote(m_send.at[pl.ds(far, 4)], m_recv.at[pl.ds(far, 4)], sib)),
        go(remote(m_send.at[pl.ds(near, 4)], m_recv.at[pl.ds(near, 4)], sib)),
    ]

    input_grad(1)

    m_copies[0].wait_recv()
    for j in range(4):
        xsend[j] = (m_own[far + j] + m_recv[far + j].astype(F32)).astype(BF)
    x_copy = go(remote(xsend, xrecv, across))
    b_copy.wait_recv()
    b_own[0] = b_own[0] + b_recv[:, 0:WT].astype(F32)
    half = b_own[0, pl.ds(pl.multiple_of((1 - xh) * HALF, 8), HALF), :]
    bxs[:, 0:WT] = jnp.concatenate([half, jnp.zeros((HPAD - HALF, WT), F32)], axis=0).astype(BF)
    bx_copy = go(remote(bxs, bxr, across))

    def finish(w):
        for copy in rs[w]:
            copy.wait_recv()
        total = tsh[WT * w : WT * (w + 1), :] + rs_send[w, chip].astype(F32)
        for k in range(CHIPS - 1):
            total = total + rs_recv[w, k].astype(F32)
        fin[WT * w : WT * (w + 1), :] = total
        fsend[WT * w : WT * (w + 1), :] = total.astype(BF)

    finish(0)
    f_copies = [go(remote(fsend.at[0:WT], frecv.at[0:WT], sib))]

    m_copies[1].wait_recv()
    x_copy.wait_recv()
    for j in range(4):
        total = m_own[near + j] + m_recv[near + j].astype(F32) + xrecv[j].astype(F32)
        top, bottom = total[0:128], total[128:256]
        even = jnp.where(low, top, pltpu.roll(bottom, HD, 1))
        odd = jnp.where(low, pltpu.roll(top, HD, 1), bottom)
        zown[2 * j, 0:128, :] = even
        zown[2 * j + 1, 0:128, :] = odd
    bx_copy.wait_recv()
    half = b_own[0, pl.ds(pl.multiple_of(xh * HALF, 8), HALF), :] + bxr[...].astype(F32)[0:HALF, 0:WT]
    b_own[1, 0:HALF, :] = half
    for i in range(ZL):
        rows = b_own[1, 9 * i : 9 * (i + 1), :]
        zown[i, 128:137, :] = rows[:, 0:128]
        zown[i, 144:153, 0:16] = rows[:, 128:144]
    zsend[...] = zown[...].astype(BF)
    z_copies = []
    for k in range(1, ZL):
        to = lax.rem(z + k, ZL)
        z_copies.append(go(remote(zsend.at[to], zrecv.at[k - 1], zs[k])))

    finish(1)
    f_copies.append(go(remote(fsend.at[WT : WT + HPAD], frecv.at[WT : WT + HPAD], sib)))
    fhs[...] = jnp.concatenate(
        [fin[NT - HALF : NT, :], jnp.zeros((HPAD - HALF, 128), F32)], axis=0
    ).astype(BF)
    f_copies.append(go(remote(fhs, fhr0, up_same)))
    f_copies.append(go(remote(fhs, fhr1, up_cross)))

    for copy in z_copies:
        copy.wait_recv()
    total = zown[z]
    for k in range(ZL - 1):
        total = total + zrecv[k].astype(F32)
    main = total[0:128]
    out_proj[...] = pltpu.roll(main, HD, 1)[HD:128, 0:HD]
    flip = main.T
    out_qkv[0] = flip[0:HD, 0:HD]
    out_qkv[1] = pltpu.roll(flip, HD, 1)[0:HD, 0:HD]
    out_qkv[2] = flip[HD:128, 0:HD]
    out_bias[0, :, 0:128] = total[128:137]
    out_bias[0, :, 128:144] = total[144:153, 0:16]

    for copy in f_copies:
        copy.wait_recv()

    def chosen(x):
        return jnp.where(core == 0, x, pltpu.roll(x, HD, 1))

    outf[0, 0:HALF, :] = chosen(fhr0[...].astype(F32))[0:HALF]
    outf[0, HALF:NT, :] = chosen(fin[0 : NT - HALF, :])
    outf[1, 0:HALF, :] = chosen(fhr1[...].astype(F32))[0:HALF]
    outf[1, HALF:NT, :] = chosen(frecv[...].astype(F32))[0 : NT - HALF]
    for i in range(2):
        r = core if i == 0 else 1 - core
        for l in range(LON):
            out_in[l, r] = outf[i, CELLS * l : CELLS * (l + 1), 0:HD].astype(BF)

    for copy in started:
        copy.wait_send()


def per_device(activations, qkv_weight, proj_weight, pos_bias, out_grad):
    v = pltpu.VMEM
    scratch = [
        v((LON, CELLS, D), BF),
        v((LON, ROWS, CELLS, HD), BF),
        v((3, D, HD), BF),
        v((HD, D), BF),
        v((1, WT, WT), F32),
        v((NT, D), F32),
        v((HPAD, D), F32),
        v((HPAD, D), BF),
        v((HPAD, D), BF),
        v((NT, D), F32),
        v((NT, D), BF),
        v((NT, 128), F32),
        v((NT, 128), F32),
        v((NT, 128), BF),
        v((NT, 128), BF),
        v((NT, 128), F32),
        v((HPAD, 128), BF),
        v((HPAD, 128), BF),
        v((1536, 128), BF),
        v((1536, 128), BF),
        v((HD, D), BF),
        v((1, WT, WT), F32),
        v((D, 384), BF),
        v((128, D), BF),
        v((2, CHIPS, WT, 128), BF),
        v((NT, 384), BF),
        v((2, 2, WT, WT), F32),
        v((NT, 128), BF),
        v((NT, 384), BF),
        v((CHIPS, 256, 128), F32),
        v((CHIPS, 256, 128), BF),
        v((CHIPS, 256, 128), BF),
        v((2, WT, WT), F32),
        v((WT, 256), BF),
        v((WT, 256), BF),
        v((4, 256, 128), BF),
        v((4, 256, 128), BF),
        v((HPAD, 256), BF),
        v((HPAD, 256), BF),
        v((ZL, 160, 128), F32),
        v((ZL, 160, 128), BF),
        v((ZL - 1, 160, 128), BF),
        v((2, CHIPS, WT, 128), BF),
        v((2, CHIPS - 1, WT, 128), BF),
        v((NT, 128), F32),
        v((NT, 128), BF),
        v((WT + HPAD, 128), BF),
        v((HPAD, 128), BF),
        v((HPAD, 128), BF),
        v((HPAD, 128), BF),
        v((2, NT, 128), F32),
        pltpu.SemaphoreType.DMA((5,)),
        pltpu.SemaphoreType.DMA((56,)),
        pltpu.SemaphoreType.DMA((56,)),
    ]
    hbm = pl.BlockSpec(memory_space=pl.ANY)
    vmem = pl.BlockSpec(memory_space=pltpu.VMEM)
    return pl.pallas_call(
        kernel,
        out_shape=(
            jax.ShapeDtypeStruct((LON, ROWS, CELLS, HD), BF),
            jax.ShapeDtypeStruct((3, HD, HD), F32),
            jax.ShapeDtypeStruct((HD, HD), F32),
            jax.ShapeDtypeStruct((1, 9, WT), F32),
        ),
        in_specs=[hbm] * 5,
        out_specs=(vmem,) * 4,
        scratch_shapes=scratch,
        compiler_params=pltpu.CompilerParams(
            collective_id=0, has_side_effects=True, vmem_limit_bytes=48 << 20
        ),
    )(activations, qkv_weight, proj_weight, pos_bias, out_grad)


def solution(mesh):
    placed = (
        P("lon", None, None, None),
        P(None, None, "tp"),
        P("tp", None),
        P("tp", None, None),
        P("lon", None, None, "tp"),
    )
    return jax.shard_map(
        per_device,
        mesh=mesh,
        in_specs=placed,
        out_specs=(
            P("lon", None, None, "tp"),
            P(None, "lon", "tp"),
            P("tp", "lon"),
            P("tp", "lon", None),
        ),
        check_vma=False,
    )
```

time: 631 us -> 54 us (0.09)
  waiting for transfers between devices: 470 us -> 0 us
  blocking collectives: 60.9 us -> 0 us
  Pallas kernels: 0 us -> 47.2 us
  local copies, waits for them, and re-layouts: 36.2 us -> 6 us
  other arithmetic: 19.7 us -> 0 us
  starting transfers between devices: 15.1 us -> 0 us
  between operations: 14.8 us -> 0.69 us
  matrix products: 13.3 us -> 0 us
    unnamed x6 -> x0, waiting for transfers between devices: 302 us -> none
    psum x1 -> x0, waiting for transfers between devices: 129 us -> none  [per_device(): summed = lax.psum(pending.astype(jnp.bfloat16), 'tp').astype(jnp.float32)]
    unnamed x1 -> x0, blocking collectives: 60.9 us -> none
    pallas_call x0 -> x1, Pallas kernels: none -> 47.2 us  [per_device(): pl.pallas_call(kernel, out_shape=(jax.ShapeDtypeStruct((LON, ROWS, CELLS,...]
    all_gather x1 -> x0, waiting for transfers between devices: 24.9 us -> none  [per_device(): grad_shift = lax.all_gather(grad_local, 'tp', axis=3, tiled=True)]
    all_gather x1 -> x0, local copies, waits for them, and re-layouts: 15.6 us -> none  [per_device(): grad_shift = lax.all_gather(grad_local, 'tp', axis=3, tiled=True)]
    ppermute x3 -> x0, starting transfers between devices: 14.9 us -> none  [shifted_2(): lax.ppermute(x, axis, [(i, (i + by) % length) for i in range(length)])]
    ppermute x3 -> x0, waiting for transfers between devices: 14 us -> none  [shifted_2(): lax.ppermute(x, axis, [(i, (i + by) % length) for i in range(length)])]
  transfers between devices with their start and end apart: 7 -> 0, of which waited for: 6 -> 0; matrix products, arithmetic and copies ran while one was open for 5% -> 0% of each run, Pallas kernels for 0% -> 0%
where the time goes in v1:
time: 54 us; the launch traced here: 53.9 us
  Pallas kernels  47.2 us (87%)
  local copies, waits for them, and re-layouts  6 us (11%)
  between operations  0.69 us (1%)
    pallas_call x1, Pallas kernels, per_device(): pl.pallas_call(kernel, out_shape=(jax.ShapeDtypeStruct((LON, ROWS, CELLS,...  47.2 us
    unnamed x11, local copies, waits for them, and re-layouts  4.62 us
    pallas_call x2, local copies, waits for them, and re-layouts, per_device(): pl.pallas_call(kernel, out_shape=(jax.ShapeDtypeStruct((LON, ROWS, CELLS,...  1.38 us

profile of v1, /device:TPU:1, one launch (start us, length us, event | category | flops | bytes accessed | tf_op | source)
XLA Modules:
  0.0 53.9 jit_solution(16658747612865067195)
XLA Ops:
  0.6 0.0 copy-start.2
  0.6 1.0 %copy.11.og = bf16[24,2,12,64]{3,2,1,0:T(8,128)(2,1)S(1)} copy(bf16[24,2,12,64]{3,1,2,0:T(2,128)(2,1)} %param.9) | data formatting | bytes 147456 | tf_op args[4]
  1.7 1.4 %copy.10.qw = bf16[3,1024,64]{2,1,0:T(8,128)(2,1)S(1)} copy(bf16[3,1024,64]{1,2,0:T(8,128)(2,1)} %param.6) | data formatting | bytes 786432 | tf_op args[1]
  3.1 0.0 copy-done.2
  3.1 0.0 copy-start
  3.1 0.0 copy-start.1
  3.1 0.3 copy.9.act
  3.4 0.5 copy-done
  4.0 0.1 copy-done.1
  4.0 47.2 %shard_map.84 = (bf16[24,2,12,64]{3,2,1,0:T(8,128)(2,1)S(1)}, f32[3,64,64]{2,1,0:T(8,128)S(1)}, f32[64,64]{1,0:T(8,128)S(1)}, f32[1,9,144]{2,1,0:T(8,128)S(1)}) custom-call(bf16[24,2,12,1024]{3,2,1,0:T(8,128)(2,1)S(1)} %copy.9.act, bf16[3,1024,64]{2,1,0:T(8,128)(2,1)S(1)} %copy.10.qw, bf16[64,1024]{1,0:T(8,128)(2,1)S(1)} %copy-done.1, ...), custom_call_target="tpu_custom_call" | custom-call | tf_op jit(solution)/shard_map/pallas_call | solution.py:493
  51.2 0.8 %copy.12 = bf16[24,2,12,64]{3,1,2,0:T(2,128)(2,1)} copy(bf16[24,2,12,64]{3,2,1,0:T(8,128)(2,1)S(1)} %get-tuple-element.4) | data formatting | bytes 147456 | tf_op jit(solution)/shard_map/pallas_call | solution.py:493
  52.0 0.6 %copy.13 = f32[1,9,144]{2,0,1:T(1,128)} copy(f32[1,9,144]{2,1,0:T(8,128)S(1)} %get-tuple-element.7) | data formatting | bytes 10368 | tf_op jit(solution)/shard_map/pallas_call | solution.py:493
  52.6 0.6 %copy.16 = f32[3,64,64]{2,1,0:T(8,128)} copy(f32[3,64,64]{2,1,0:T(8,128)S(1)} %get-tuple-element.13) | data formatting | bytes 98304
  53.2 0.6 %copy.17 = f32[64,64]{1,0:T(8,128)} copy(f32[64,64]{1,0:T(8,128)S(1)} %get-tuple-element.14) | data formatting | bytes 32768
Async XLA Ops:
  0.6 2.4 %copy-start.2 = (bf16[24,2,12,1024]{3,1,2,0:T(2,128)(2,1)S(1)}, bf16[24,2,12,1024]{3,1,2,0:T(2,128)(2,1)}, u32[]{:S(2)}) copy-start(bf16[24,2,12,1024]{3,1,2,0:T(2,128)(2,1)} %param.5) | copy-start | bytes 3538948
  3.1 0.9 %copy-start = (f32[1,144,144]{2,1,0:T(8,128)S(1)}, f32[1,144,144]{2,1,0:T(8,128)}, u32[]{:S(2)}) copy-start(f32[1,144,144]{2,1,0:T(8,128)} %pb.1) | copy-start | bytes 248836
  3.1 1.0 %copy-start.1 = (bf16[64,1024]{1,0:T(8,128)(2,1)S(1)}, bf16[64,1024]{1,0:T(8,128)(2,1)}, u32[]{:S(2)}) copy-start(bf16[64,1024]{1,0:T(8,128)(2,1)} %pw.1) | copy-start | bytes 393220

commit v2 on v1

v2 whole, which is shorter than its diff:
```python
import jax
import jax.numpy as jnp
from jax import lax
from jax.experimental import pallas as pl
from jax.experimental.pallas import tpu as pltpu
from jax.sharding import PartitionSpec as P

BF = jnp.bfloat16
F32 = jnp.float32
MESH = pl.DeviceIdType.MESH

LON = 24
ROWS = 2
CELLS = 12
D = 1024
HD = 64
WT = 144
NT = 288
HALF = 72
HPAD = 80
CHIPS = 8
ZL = 8
SCALE = 0.125


def nt(a, b):
    return lax.dot_general(a, b, (((1,), (1,)), ((), ())), preferred_element_type=F32)


def tn(a, b):
    return lax.dot_general(a, b, (((0,), (0,)), ((), ())), preferred_element_type=F32)


def nn(a, b):
    return jnp.dot(a, b, preferred_element_type=F32)


def kernel(
    act,
    qw,
    pw,
    pb,
    og,
    out,
    act_v,
    og_v,
    xs,
    hs,
    hsend,
    hrecv,
    nf,
    xb,
    inv_s,
    pf,
    psend,
    precv,
    tsh,
    tsend,
    trecv,
    w2,
    pw2,
    pb2,
    g,
    qkv_s,
    probs_s,
    att_s,
    dqkv_s,
    ma_own,
    ma_send,
    ma_recv,
    mb_own,
    mb_send,
    mb_recv,
    b_own,
    b_send,
    b_recv,
    xa_send,
    xa_recv,
    bx_send,
    bx_recv,
    za_own,
    za_send,
    za_recv,
    zb_own,
    zb_send,
    zb_recv,
    xb_send,
    xb_recv,
    rs_send,
    rs_recv,
    fin,
    fsend,
    frecv,
    fhs,
    fhr0,
    fhr1,
    lsem,
    ssem,
    rsem,
):
    tp = lax.axis_index("tp")
    lon = lax.axis_index("lon")
    core = lax.rem(tp, 2)
    chip = lax.div(tp, 2)
    xh = lax.div(lon, ZL)
    z = lax.rem(lon, ZL)
    sib_tp = chip * 2 + 1 - core
    up = lax.rem(lon + 1, 16)
    down = lax.rem(lon + 15, 16)
    sib = {"tp": sib_tp}
    down_same = {"lon": down}
    up_same = {"lon": up}
    up_cross = {"lon": up, "tp": sib_tp}
    down_cross = {"lon": down, "tp": sib_tp}
    across = {"lon": (1 - xh) * ZL + z}
    chips = [None] + [{"tp": lax.rem(chip + k, CHIPS) * 2 + core} for k in range(1, CHIPS)]
    zs = [None] + [{"lon": xh * ZL + lax.rem(z + k, ZL)} for k in range(1, ZL)]

    barrier = pltpu.get_barrier_semaphore()
    peers = [sib] + chips[1:] + [down_same, up_same, up_cross, down_cross, across] + zs[1:]
    for peer in peers:
        pl.semaphore_signal(barrier, inc=1, device_id=peer, device_id_type=MESH)

    loads = [
        pltpu.make_async_copy(og, og_v, lsem.at[0]),
        pltpu.make_async_copy(qw, w2.at[:, 0], lsem.at[1]),
        pltpu.make_async_copy(pw, pw2.at[0], lsem.at[2]),
        pltpu.make_async_copy(pb.at[0], pb2.at[0], lsem.at[3]),
        pltpu.make_async_copy(act, act_v, lsem.at[4]),
    ]
    for load in loads:
        load.start()

    count = [0]

    def remote(src, dst, peer):
        i = count[0]
        count[0] += 1
        return pltpu.make_async_remote_copy(
            src_ref=src,
            dst_ref=dst,
            send_sem=ssem.at[i],
            recv_sem=rsem.at[i],
            device_id=peer,
            device_id_type=MESH,
        )

    started = []

    def go(copy):
        copy.start()
        started.append(copy)
        return copy

    low = lax.broadcasted_iota(jnp.int32, (1, 128), 1) < HD

    loads[0].wait()
    for l in range(LON):
        both = og_v[l].astype(F32)
        pf[CELLS * l : CELLS * (l + 1), :] = jnp.concatenate([both[:, 0], both[:, 1]], axis=1)
    psend[...] = pf[...].astype(BF)

    pl.semaphore_wait(barrier, len(peers))

    p_copy = go(remote(psend, precv, sib))
    for load in loads[1:4]:
        load.wait()
    w_copy = go(remote(w2.at[:, 0], w2.at[:, 1], sib))
    pw_copy = go(remote(pw2.at[0], pw2.at[1], sib))
    pb_copy = go(remote(pb2.at[0], pb2.at[1], sib))

    loads[4].wait()

    def row_of(l):
        both = act_v[l].astype(F32)
        return jnp.where(core == 0, both[:, 0], both[:, 1])

    for l in range(6):
        hs[CELLS * l : CELLS * (l + 1), :] = row_of(l)
    hs[HALF:HPAD, :] = jnp.zeros((HPAD - HALF, D), F32)
    hsend[...] = hs[...].astype(BF)
    h_copy = go(remote(hsend, hrecv, down_same))

    p_copy.wait_recv()
    mine = low == (core == 0)
    merged = jnp.where(mine, pf[...], pltpu.roll(precv[...].astype(F32), HD, 1))
    tsend[...] = merged[0:HPAD].astype(BF)
    t_copy = go(remote(tsend, trecv, down_same))
    tsh[0 : NT - HALF, :] = merged[HALF:NT]
    g[0, chip] = merged[HALF : HALF + WT].astype(BF)
    ag = [[], []]
    for k in range(1, CHIPS):
        ag[0].append(go(remote(g.at[0, chip], g.at[0, chip], chips[k])))

    for l in range(6, LON):
        xs[CELLS * (l - 6) : CELLS * (l - 5), :] = row_of(l)

    def norm(w):
        def body(i, carry):
            r = pl.ds(pl.multiple_of(WT * w + 48 * i, 16), 48)
            x = xs[r, :]
            cen = x - jnp.mean(x, axis=1, keepdims=True)
            inv = lax.rsqrt(jnp.mean(cen * cen, axis=1, keepdims=True) + 1e-05)
            y = cen * inv
            nf[r, :] = y
            xb[r, :] = y.astype(BF)
            inv_s[r, :] = jnp.broadcast_to(inv, (48, 128))
            return carry

        lax.fori_loop(0, 3, body, 0)

    t_copy.wait_recv()
    tsh[NT - HALF : NT, :] = trecv[...].astype(F32)[0:HALF]
    g[1, chip] = tsh[WT:NT, :].astype(BF)
    for k in range(1, CHIPS):
        ag[1].append(go(remote(g.at[1, chip], g.at[1, chip], chips[k])))

    norm(0)
    w_copy.wait_recv()
    pw_copy.wait_recv()
    pb_copy.wait_recv()

    def weights():
        return w2[...].reshape(6 * HD, D)

    wsum = nt(jnp.ones((8, D), BF), weights())[0:1]

    def forward(w):
        r = pl.ds(WT * w, WT)
        qkv = nt(xb[r, :], weights()).astype(BF)
        qkv_s[r, :] = qkv
        q2, k2, v2 = qkv[:, 0:128], qkv[:, 128:256], qkv[:, 256:384]
        att = []
        for h in range(2):
            keep = low if h == 0 else jnp.logical_not(low)
            s = nt(jnp.where(keep, q2, jnp.zeros_like(q2)), k2) * SCALE + pb2[h]
            e = jnp.exp(s - jnp.max(s, axis=1, keepdims=True))
            p = e * (1.0 / jnp.sum(e, axis=1, keepdims=True))
            probs_s[w, h] = p
            att.append(nn(p.astype(BF), v2))
        att_s[r, :] = jnp.where(low, att[0], att[1]).astype(BF)

    forward(0)

    h_copy.wait_recv()
    xs[NT - HALF : NT, :] = hrecv[...].astype(F32)[0:HALF]
    norm(1)
    forward(1)

    def backward(w):
        r = pl.ds(WT * w, WT)
        grads = jnp.concatenate([g[w, m] for m in range(CHIPS)], axis=1)
        ga = nt(grads, pw2[...].reshape(2 * HD, D)).astype(BF)
        q2, k2, v2 = qkv_s[r, 0:128], qkv_s[r, 128:256], qkv_s[r, 256:384]
        dq, dk, dv = [], [], []
        for h in range(2):
            keep = low if h == 0 else jnp.logical_not(low)
            p = probs_s[w, h]
            gp = nt(jnp.where(keep, ga, jnp.zeros_like(ga)), v2)
            ds = p * (gp - jnp.sum(gp * p, axis=1, keepdims=True))
            if w == 0:
                b_own[h] = ds
            else:
                b_own[h] = b_own[h] + ds
            dl = ds.astype(BF)
            dv.append(tn(p.astype(BF), ga))
            dq.append(nn(dl, k2) * SCALE)
            dk.append(tn(dl, q2) * SCALE)
        dqkv_s[r, 0:128] = jnp.where(low, dq[0], dq[1]).astype(BF)
        dqkv_s[r, 128:256] = jnp.where(low, dk[0], dk[1]).astype(BF)
        dqkv_s[r, 256:384] = jnp.where(low, dv[0], dv[1]).astype(BF)

    rs = [[], []]

    def input_grad(w):
        r = pl.ds(WT * w, WT)
        dq = dqkv_s[r, :]
        wide = dq.astype(F32)
        inv = inv_s[r, 0:1]
        first = jnp.sum(wide * wsum, axis=1, keepdims=True) * (1.0 / D)
        second = jnp.sum(wide * qkv_s[r, :].astype(F32), axis=1, keepdims=True) * (1.0 / D)
        for m in range(CHIPS):
            lanes = slice(128 * m, 128 * (m + 1))
            part = nn(dq, w2[:, :, :, lanes].reshape(6 * HD, 128))
            part = inv * (part - first - nf[r, lanes] * second)
            rs_send[w, m] = part.astype(BF)
        for k in range(1, CHIPS):
            to = lax.rem(chip + k, CHIPS)
            rs[w].append(go(remote(rs_send.at[w, to], rs_recv.at[w, k - 1], chips[k])))

    for copy in ag[0]:
        copy.wait_recv()
    backward(0)
    input_grad(0)

    for copy in ag[1]:
        copy.wait_recv()
    backward(1)

    def weight_grad(parts, own, send):
        for m in range(CHIPS):
            for i, c in enumerate(parts):
                if c < 3:
                    left, right = dqkv_s[:, 128 * c : 128 * (c + 1)], xb[:, 128 * m : 128 * (m + 1)]
                else:
                    left = att_s[...]
                    right = jnp.concatenate([g[0, m], g[1, m]], axis=0)
                part = tn(left, right)
                own[m, HD * i : HD * (i + 1), :] = part[0:HD]
                send[m, HD * i : HD * (i + 1), :] = part[HD:128].astype(BF)

    weight_grad((1, 3), mb_own, mb_send)
    mb_copy = go(remote(mb_send, mb_recv, sib))
    b_send[:, 0:WT] = b_own[1].astype(BF)
    b_copy = go(remote(b_send, b_recv, sib))
    weight_grad((0, 2), ma_own, ma_send)
    far = (1 - xh) * 4
    near = xh * 4
    ma_copies = [
        go(remote(ma_send.at[pl.ds(i, 4)], ma_recv.at[pl.ds(i, 4)], sib)) for i in (far, near)
    ]

    def packed(total):
        top, bottom = total[0:HD], total[HD:128]
        return (
            jnp.where(low, top, pltpu.roll(bottom, HD, 1)),
            jnp.where(low, pltpu.roll(top, HD, 1), bottom),
        )

    mb_copy.wait_recv()
    for m in range(CHIPS):
        even, odd = packed(mb_own[m] + mb_recv[m].astype(F32))
        to = (2 * m) % ZL
        zb_own[to, m // 4] = even
        zb_own[to + 1, m // 4] = odd
        zb_send[to, m // 4] = even.astype(BF)
        zb_send[to + 1, m // 4] = odd.astype(BF)
    zb_copies = []
    for k in range(1, ZL):
        to = lax.rem(z + k, ZL)
        zb_copies.append(go(remote(zb_send.at[to], zb_recv.at[k - 1], zs[k])))

    ma_copies[0].wait_recv()
    for j in range(4):
        xa_send[j] = (ma_own[far + j] + ma_recv[far + j].astype(F32)).astype(BF)
    xa_copy = go(remote(xa_send, xa_recv, across))
    b_copy.wait_recv()
    b_own[0] = b_own[0] + b_recv[:, 0:WT].astype(F32)
    half = b_own[0, pl.ds(pl.multiple_of((1 - xh) * HALF, 8), HALF), :]
    bx_send[:, 0:WT] = jnp.concatenate([half, jnp.zeros((HPAD - HALF, WT), F32)], axis=0).astype(BF)
    bx_copy = go(remote(bx_send, bx_recv, across))

    input_grad(1)

    def finish(w):
        for copy in rs[w]:
            copy.wait_recv()
        total = tsh[WT * w : WT * (w + 1), :] + rs_send[w, chip].astype(F32)
        for k in range(CHIPS - 1):
            total = total + rs_recv[w, k].astype(F32)
        fin[WT * w : WT * (w + 1), :] = total
        fsend[WT * w : WT * (w + 1), :] = total.astype(BF)

    finish(0)
    f_copies = [go(remote(fsend.at[0:WT], frecv.at[0:WT], sib))]
    finish(1)
    fhs[...] = jnp.concatenate(
        [fin[NT - HALF : NT, :], jnp.zeros((HPAD - HALF, 128), F32)], axis=0
    ).astype(BF)
    f_copies.append(go(remote(fhs, fhr0, up_same)))
    f_copies.append(go(remote(fhs, fhr1, up_cross)))
    f_copies.append(go(remote(fsend.at[WT : WT + HPAD], frecv.at[WT : WT + HPAD], sib)))

    ma_copies[1].wait_recv()
    xa_copy.wait_recv()
    for j in range(4):
        even, odd = packed(ma_own[near + j] + ma_recv[near + j].astype(F32) + xa_recv[j].astype(F32))
        za_own[2 * j, 0:HD, :] = even
        za_own[2 * j + 1, 0:HD, :] = odd
    bx_copy.wait_recv()
    half = b_own[0, pl.ds(pl.multiple_of(xh * HALF, 8), HALF), :]
    b_own[1, 0:HALF, :] = half + bx_recv[...].astype(F32)[0:HALF, 0:WT]
    for i in range(ZL):
        rows = b_own[1, 9 * i : 9 * (i + 1), :]
        za_own[i, HD : HD + 9, :] = rows[:, 0:128]
        za_own[i, HD + 16 : HD + 25, 0:16] = rows[:, 128:144]
    za_send[...] = za_own[...].astype(BF)
    za_copies = []
    for k in range(1, ZL):
        to = lax.rem(z + k, ZL)
        za_copies.append(go(remote(za_send.at[to], za_recv.at[k - 1], zs[k])))

    for copy in zb_copies:
        copy.wait_recv()

    def over_z(part):
        total = zb_own[z, part]
        for k in range(ZL - 1):
            total = total + zb_recv[k, part].astype(F32)
        return total

    xb_send[...] = over_z(1 - xh).astype(BF)
    xb_copy = go(remote(xb_send, xb_recv, across))
    second_half = over_z(xh)

    for copy in f_copies:
        copy.wait_recv()

    def chosen(x):
        return jnp.where(core == 0, x, pltpu.roll(x, HD, 1))

    here = jnp.concatenate([chosen(fhr0[...].astype(F32))[0:HALF], chosen(fin[0 : NT - HALF, :])], axis=0)
    there = jnp.concatenate(
        [chosen(fhr1[...].astype(F32))[0:HALF], chosen(frecv[...].astype(F32))[0 : NT - HALF]], axis=0
    )
    out[0:NT, :] = jnp.where(
        low, jnp.where(core == 0, here, there), pltpu.roll(jnp.where(core == 0, there, here), HD, 1)
    )

    xb_copy.wait_recv()
    out[NT : NT + HD, :] = second_half + xb_recv[...].astype(F32)

    for copy in za_copies:
        copy.wait_recv()
    total = za_own[z]
    for k in range(ZL - 1):
        total = total + za_recv[k].astype(F32)
    out[NT + HD : NT + HD + 96, :] = total

    for copy in started:
        copy.wait_send()


def unpack(parts, out_in, out_qkv, out_proj, out_bias):
    for l in range(LON):
        x = parts[CELLS * l : CELLS * (l + 1), :]
        out_in[l] = jnp.stack([x[:, 0:HD], x[:, HD:128]], axis=1).astype(BF)
    key_proj = parts[NT : NT + HD, :]
    query_value = parts[NT + HD : NT + 2 * HD, :].T
    out_qkv[0] = query_value[0:HD]
    out_qkv[1] = key_proj.T[0:HD]
    out_qkv[2] = query_value[HD:128]
    out_proj[...] = pltpu.roll(key_proj, HD, 1)[:, 0:HD]
    at = NT + 2 * HD
    out_bias[:, 0, 0:128] = parts[at : at + 9, :]
    out_bias[:, 0, 128:144] = parts[at + 16 : at + 25, 0:16]


def per_device(activations, qkv_weight, proj_weight, pos_bias, out_grad):
    v = pltpu.VMEM
    scratch = [
        v((LON, CELLS, ROWS, D), BF),
        v((LON, CELLS, ROWS, HD), BF),
        v((NT, D), F32),
        v((HPAD, D), F32),
        v((HPAD, D), BF),
        v((HPAD, D), BF),
        v((NT, D), F32),
        v((NT, D), BF),
        v((NT, 128), F32),
        v((NT, 128), F32),
        v((NT, 128), BF),
        v((NT, 128), BF),
        v((NT, 128), F32),
        v((HPAD, 128), BF),
        v((HPAD, 128), BF),
        v((3, 2, HD, D), BF),
        v((2, HD, D), BF),
        v((2, WT, WT), F32),
        v((2, CHIPS, WT, 128), BF),
        v((NT, 384), BF),
        v((2, 2, WT, WT), F32),
        v((NT, 128), BF),
        v((NT, 384), BF),
        v((CHIPS, 128, 128), F32),
        v((CHIPS, 128, 128), BF),
        v((CHIPS, 128, 128), BF),
        v((CHIPS, 128, 128), F32),
        v((CHIPS, 128, 128), BF),
        v((CHIPS, 128, 128), BF),
        v((2, WT, WT), F32),
        v((WT, 256), BF),
        v((WT, 256), BF),
        v((4, 128, 128), BF),
        v((4, 128, 128), BF),
        v((HPAD, 256), BF),
        v((HPAD, 256), BF),
        v((ZL, 96, 128), F32),
        v((ZL, 96, 128), BF),
        v((ZL - 1, 96, 128), BF),
        v((ZL, 2, HD, 128), F32),
        v((ZL, 2, HD, 128), BF),
        v((ZL - 1, 2, HD, 128), BF),
        v((HD, 128), BF),
        v((HD, 128), BF),
        v((2, CHIPS, WT, 128), BF),
        v((2, CHIPS - 1, WT, 128), BF),
        v((NT, 128), F32),
        v((NT, 128), BF),
        v((WT + HPAD, 128), BF),
        v((HPAD, 128), BF),
        v((HPAD, 128), BF),
        v((HPAD, 128), BF),
        pltpu.SemaphoreType.DMA((5,)),
        pltpu.SemaphoreType.DMA((64,)),
        pltpu.SemaphoreType.DMA((64,)),
    ]
    hbm = pl.BlockSpec(memory_space=pl.ANY)
    vmem = pl.BlockSpec(memory_space=pltpu.VMEM)
    shapes = (
        jax.ShapeDtypeStruct((LON, CELLS, ROWS, HD), BF),
        jax.ShapeDtypeStruct((3, HD, HD), F32),
        jax.ShapeDtypeStruct((HD, HD), F32),
        jax.ShapeDtypeStruct((9, 1, WT), F32),
    )
    parts = pl.pallas_call(
        kernel,
        out_shape=jax.ShapeDtypeStruct((NT + HD + 96, 128), F32),
        in_specs=[hbm] * 5,
        out_specs=vmem,
        scratch_shapes=scratch,
        compiler_params=pltpu.CompilerParams(
            collective_id=0, has_side_effects=True, vmem_limit_bytes=60 << 20
        ),
    )(
        activations.transpose(0, 2, 1, 3),
        qkv_weight.transpose(0, 2, 1),
        proj_weight,
        pos_bias,
        out_grad.transpose(0, 2, 1, 3),
    )
    in_grad, qkv_grad, proj_grad, bias_grad = pl.pallas_call(
        unpack,
        out_shape=shapes,
        in_specs=[vmem],
        out_specs=(vmem,) * 4,
        compiler_params=pltpu.CompilerParams(vmem_limit_bytes=60 << 20),
    )(parts)
    return in_grad.transpose(0, 2, 1, 3), qkv_grad, proj_grad, bias_grad.transpose(1, 0, 2)


def solution(mesh):
    placed = (
        P("lon", None, None, None),
        P(None, None, "tp"),
        P("tp", None),
        P("tp", None, None),
        P("lon", None, None, "tp"),
    )
    return jax.shard_map(
        per_device,
        mesh=mesh,
        in_specs=placed,
        out_specs=(
            P("lon", None, None, "tp"),
            P(None, "lon", "tp"),
            P("tp", "lon"),
            P("tp", "lon", None),
        ),
        check_vma=False,
    )
```

time: 54 us -> 47.2 us (0.87)
  local copies, waits for them, and re-layouts: 6 us -> 0 us
  Pallas kernels: 47.2 us -> 46.4 us
    unnamed x11 -> x0, local copies, waits for them, and re-layouts: 4.62 us -> none
    pallas_call x2 -> x0, local copies, waits for them, and re-layouts: 1.38 us -> none  [per_device(): pl.pallas_call(kernel, out_shape=(jax.ShapeDtypeStruct((LON, ROWS, CELLS,...]
    pallas_call x1 -> x2, Pallas kernels: 47.2 us -> 46.4 us  [the longest x1 44.5 us: per_device(): pl.pallas_call(kernel, out_shape=jax.ShapeDtypeStruct((NT + HD + 96, 128)...]
where the time goes in v2:
time: 47.2 us; the launch traced here: 47.1 us
  Pallas kernels  46.4 us (98%)
  between operations  0.64 us (1%)
    pallas_call x1, Pallas kernels, per_device(): pl.pallas_call(kernel, out_shape=jax.ShapeDtypeStruct((NT + HD + 96, 128)...  44.5 us
    pallas_call x1, Pallas kernels, per_device(): pl.pallas_call(unpack, out_shape=shapes, in_specs=[vmem], out_specs=(vmem...  1.89 us

profile of v2, /device:TPU:1, one launch (start us, length us, event | category | flops | bytes accessed | tf_op | source)
XLA Modules:
  0.0 47.1 jit_solution(4058876471041068694)
XLA Ops:
  0.6 44.5 %shard_map.84.parts = f32[448,128]{1,0:T(8,128)} custom-call(bf16[24,12,2,1024]{3,2,1,0:T(2,128)(2,1)} %bitcast.5, bf16[3,64,1024]{2,1,0:T(8,128)(2,1)} %bitcast.6, bf16[64,1024]{1,0:T(8,128)(2,1)} %pw.1, f32[1,144,144]{2,1,0:T(8,128)} %pb.1, bf16[24,12,2,64]{3,2,1,0:T(2,128)(2,1)} %bitcast.7), custom_call_target="tpu_custom_call" | custom-call | tf_op jit(solution)/shard_map/pallas_call | solution.py:516
  45.2 1.9 %shard_map.85 = (bf16[24,12,2,64]{3,2,1,0:T(2,128)(2,1)}, f32[3,64,64]{2,1,0:T(8,128)}, f32[64,64]{1,0:T(8,128)}, f32[9,1,144]{2,1,0:T(1,128)}) custom-call(f32[448,128]{1,0:T(8,128)} %shard_map.84.parts), custom_call_target="tpu_custom_call" | custom-call | tf_op jit(solution)/shard_map/pallas_call | solution.py:532

commit v3 on v2

--- a/solution.py
+++ b/solution.py
@@ -68,9 +68,12 @@
     ma_own,
     ma_send,
     ma_recv,
-    mb_own,
-    mb_send,
-    mb_recv,
+    mk_own,
+    mk_send,
+    mk_recv,
+    mp_own,
+    mp_send,
+    mp_recv,
     b_own,
     b_send,
     b_recv,
@@ -81,13 +84,18 @@
     za_own,
     za_send,
     za_recv,
-    zb_own,
-    zb_send,
-    zb_recv,
+    zk_own,
+    zk_send,
+    zk_recv,
+    zp_own,
+    zp_send,
+    zp_recv,
     xb_send,
     xb_recv,
     rs_send,
     rs_recv,
+    rx_send,
+    rx_recv,
     fin,
     fsend,
     frecv,
@@ -114,6 +122,9 @@
     down_cross = {"lon": down, "tp": sib_tp}
     across = {"lon": (1 - xh) * ZL + z}
     chips = [None] + [{"tp": lax.rem(chip + k, CHIPS) * 2 + core} for k in range(1, CHIPS)]
+    row, side = lax.div(chip, 2), lax.rem(chip, 2)
+    ys = [None] + [{"tp": (lax.rem(row + k, 4) * 2 + side) * 2 + core} for k in range(1, 4)]
+    beside = {"tp": (row * 2 + 1 - side) * 2 + core}
     zs = [None] + [{"lon": xh * ZL + lax.rem(z + k, ZL)} for k in range(1, ZL)]
 
     barrier = pltpu.get_barrier_semaphore()
@@ -270,7 +281,18 @@
         dqkv_s[r, 128:256] = jnp.where(low, dk[0], dk[1]).astype(BF)
         dqkv_s[r, 256:384] = jnp.where(low, dv[0], dv[1]).astype(BF)
 
-    rs = [[], []]
+    early, late, halo, rest = (0, 0, 80), (0, 80, 64), (1, 64, 80), (1, 0, 64)
+    rs = {}
+
+    def send_out(part):
+        w, a, n = part
+        rows = pl.ds(a, n)
+        rs[part] = []
+        for k in range(1, 4):
+            to = lax.rem(row + k, 4)
+            rs[part].append(
+                go(remote(rs_send.at[w, to, :, rows], rs_recv.at[w, k - 1, :, rows], ys[k]))
+            )
 
     def input_grad(w):
         r = pl.ds(WT * w, WT)
@@ -283,10 +305,7 @@
             lanes = slice(128 * m, 128 * (m + 1))
             part = nn(dq, w2[:, :, :, lanes].reshape(6 * HD, 128))
             part = inv * (part - first - nf[r, lanes] * second)
-            rs_send[w, m] = part.astype(BF)
-        for k in range(1, CHIPS):
-            to = lax.rem(chip + k, CHIPS)
-            rs[w].append(go(remote(rs_send.at[w, to], rs_recv.at[w, k - 1], chips[k])))
+            rs_send[w, m // 2, m % 2] = part.astype(BF)
 
     for copy in ag[0]:
         copy.wait_recv()
@@ -295,7 +314,7 @@
 
     for copy in ag[1]:
         copy.wait_recv()
-    backward(1)
+    send_out(late)
 
     def weight_grad(parts, own, send):
         for m in range(CHIPS):
@@ -309,8 +328,12 @@
                 own[m, HD * i : HD * (i + 1), :] = part[0:HD]
                 send[m, HD * i : HD * (i + 1), :] = part[HD:128].astype(BF)
 
-    weight_grad((1, 3), mb_own, mb_send)
-    mb_copy = go(remote(mb_send, mb_recv, sib))
+    weight_grad((3,), mp_own, mp_send)
+    mp_copy = go(remote(mp_send, mp_recv, sib))
+    backward(1)
+
+    input_grad(1)
+    send_out(halo)
     b_send[:, 0:WT] = b_own[1].astype(BF)
     b_copy = go(remote(b_send, b_recv, sib))
     weight_grad((0, 2), ma_own, ma_send)
@@ -327,49 +350,83 @@
             jnp.where(low, pltpu.roll(top, HD, 1), bottom),
         )
 
-    mb_copy.wait_recv()
-    for m in range(CHIPS):
-        even, odd = packed(mb_own[m] + mb_recv[m].astype(F32))
-        to = (2 * m) % ZL
-        zb_own[to, m // 4] = even
-        zb_own[to + 1, m // 4] = odd
-        zb_send[to, m // 4] = even.astype(BF)
-        zb_send[to + 1, m // 4] = odd.astype(BF)
-    zb_copies = []
-    for k in range(1, ZL):
-        to = lax.rem(z + k, ZL)
-        zb_copies.append(go(remote(zb_send.at[to], zb_recv.at[k - 1], zs[k])))
+    def start_z(copy, own, recv, z_own, z_send, z_recv):
+        copy.wait_recv()
+        for m in range(4):
+            first = own[m] + recv[m].astype(F32)
+            second = own[m + 4] + recv[m + 4].astype(F32)
+            even = jnp.where(low, first, pltpu.roll(second, HD, 1))
+            odd = jnp.where(low, pltpu.roll(first, HD, 1), second)
+            z_own[2 * m] = even
+            z_own[2 * m + 1] = odd
+            z_send[2 * m] = even.astype(BF)
+            z_send[2 * m + 1] = odd.astype(BF)
+        out = []
+        for k in range(1, ZL):
+            to = lax.rem(z + k, ZL)
+            out.append(go(remote(z_send.at[to], z_recv.at[k - 1], zs[k])))
+        return out
+
+    zp_copies = start_z(mp_copy, mp_own, mp_recv, zp_own, zp_send, zp_recv)
+    weight_grad((1,), mk_own, mk_send)
+    mk_copy = go(remote(mk_send, mk_recv, sib))
+    send_out(early)
+    send_out(rest)
 
     ma_copies[0].wait_recv()
     for j in range(4):
         xa_send[j] = (ma_own[far + j] + ma_recv[far + j].astype(F32)).astype(BF)
     xa_copy = go(remote(xa_send, xa_recv, across))
+    zk_copies = start_z(mk_copy, mk_own, mk_recv, zk_own, zk_send, zk_recv)
     b_copy.wait_recv()
     b_own[0] = b_own[0] + b_recv[:, 0:WT].astype(F32)
     half = b_own[0, pl.ds(pl.multiple_of((1 - xh) * HALF, 8), HALF), :]
-    bx_send[:, 0:WT] = jnp.concatenate([half, jnp.zeros((HPAD - HALF, WT), F32)], axis=0).astype(BF)
+    bx_send[0:HPAD, :] = jnp.concatenate(
+        [half[:, 0:128], jnp.zeros((HPAD - HALF, 128), F32)], axis=0
+    ).astype(BF)
+    bx_send[HPAD:96, 0:HALF] = half[:, 128:WT].T.astype(BF)
     bx_copy = go(remote(bx_send, bx_recv, across))
 
-    input_grad(1)
-
-    def finish(w):
-        for copy in rs[w]:
+
+    def over_y(part, which):
+        w, a, n = part
+        rows = slice(a, a + n)
+        total = rs_send[w, row, which, rows].astype(F32)
+        for k in range(3):
+            total = total + rs_recv[w, k, which, rows].astype(F32)
+        return total
+
+    def pass_over(part):
+        w, a, n = part
+        rows = pl.ds(a, n)
+        for copy in rs[part]:
             copy.wait_recv()
-        total = tsh[WT * w : WT * (w + 1), :] + rs_send[w, chip].astype(F32)
-        for k in range(CHIPS - 1):
-            total = total + rs_recv[w, k].astype(F32)
-        fin[WT * w : WT * (w + 1), :] = total
-        fsend[WT * w : WT * (w + 1), :] = total.astype(BF)
-
-    finish(0)
-    f_copies = [go(remote(fsend.at[0:WT], frecv.at[0:WT], sib))]
-    finish(1)
-    fhs[...] = jnp.concatenate(
-        [fin[NT - HALF : NT, :], jnp.zeros((HPAD - HALF, 128), F32)], axis=0
-    ).astype(BF)
-    f_copies.append(go(remote(fhs, fhr0, up_same)))
-    f_copies.append(go(remote(fhs, fhr1, up_cross)))
-    f_copies.append(go(remote(fsend.at[WT : WT + HPAD], frecv.at[WT : WT + HPAD], sib)))
+        rx_send[w, rows] = over_y(part, 1 - side).astype(BF)
+        return go(remote(rx_send.at[w, rows], rx_recv.at[w, rows], beside))
+
+    def finish(part, copy):
+        w, a, n = part
+        r = slice(WT * w + a, WT * w + a + n)
+        total = tsh[r, :] + over_y(part, side)
+        copy.wait_recv()
+        total = total + rx_recv[w, a : a + n].astype(F32)
+        fin[r, :] = total
+        fsend[r, :] = total.astype(BF)
+
+    rx_late = pass_over(late)
+    rx_halo = pass_over(halo)
+    finish(late, rx_late)
+    finish(halo, rx_halo)
+    moved = jnp.concatenate([fin[NT - HALF : NT, :], jnp.zeros((HPAD - HALF, 128), F32)], axis=0)
+    turned = pltpu.roll(moved, HD, 1)
+    firsts = jnp.where(low, moved[0:40], turned[40:80])
+    seconds = jnp.where(low, turned[0:40], moved[40:80])
+    mine_half = jnp.where(core == 0, firsts, seconds)
+    other_half = jnp.where(core == 0, seconds, firsts)
+    blank = jnp.zeros((8, 128), F32)
+    fhs[0] = jnp.concatenate([mine_half, blank], axis=0).astype(BF)
+    fhs[1] = jnp.concatenate([other_half, blank], axis=0).astype(BF)
+    f_copies = [go(remote(fhs.at[0], fhr0, up_same)), go(remote(fhs.at[1], fhr1, up_cross))]
 
     ma_copies[1].wait_recv()
     xa_copy.wait_recv()
@@ -379,29 +436,41 @@
         za_own[2 * j + 1, 0:HD, :] = odd
     bx_copy.wait_recv()
     half = b_own[0, pl.ds(pl.multiple_of(xh * HALF, 8), HALF), :]
-    b_own[1, 0:HALF, :] = half + bx_recv[...].astype(F32)[0:HALF, 0:WT]
+    b_own[1, 0:HALF, 0:128] = half[:, 0:128] + bx_recv[...].astype(F32)[0:HALF]
+    b_own[1, 0:HALF, 128:WT] = half[:, 128:WT] + bx_recv[HPAD:96, 0:HALF].astype(F32).T
     for i in range(ZL):
         rows = b_own[1, 9 * i : 9 * (i + 1), :]
         za_own[i, HD : HD + 9, :] = rows[:, 0:128]
-        za_own[i, HD + 16 : HD + 25, 0:16] = rows[:, 128:144]
+        za_own[i, HD + 9 : HD + 16, 0:16] = rows[0:7, 128:144]
+        za_own[i, HD + 9 : HD + 11, 16:32] = rows[7:9, 128:144]
     za_send[...] = za_own[...].astype(BF)
     za_copies = []
     for k in range(1, ZL):
         to = lax.rem(z + k, ZL)
         za_copies.append(go(remote(za_send.at[to], za_recv.at[k - 1], zs[k])))
 
-    for copy in zb_copies:
-        copy.wait_recv()
-
-    def over_z(part):
-        total = zb_own[z, part]
+    rx_early = pass_over(early)
+    rx_rest = pass_over(rest)
+    finish(early, rx_early)
+    f_copies.append(go(remote(fsend.at[0:WT], frecv.at[0:WT], sib)))
+    finish(rest, rx_rest)
+    f_copies.append(go(remote(fsend.at[WT : WT + HPAD], frecv.at[WT : WT + HPAD], sib)))
+
+    def over_z(copies, z_own, z_recv):
+        for copy in copies:
+            copy.wait_recv()
+        total = z_own[z]
         for k in range(ZL - 1):
-            total = total + zb_recv[k, part].astype(F32)
-        return total
-
-    xb_send[...] = over_z(1 - xh).astype(BF)
+            total = total + z_recv[k].astype(F32)
+        return total, pltpu.roll(total, HD, 1)
+
+    proj_sum, proj_turned = over_z(zp_copies, zp_own, zp_recv)
+    key_sum, key_turned = over_z(zk_copies, zk_own, zk_recv)
+    ahead = jnp.where(low, key_sum, proj_turned)
+    behind = jnp.where(low, key_turned, proj_sum)
+    xb_send[...] = jnp.where(xh == 0, behind, ahead).astype(BF)
     xb_copy = go(remote(xb_send, xb_recv, across))
-    second_half = over_z(xh)
+    second_half = jnp.where(xh == 0, ahead, behind)
 
     for copy in f_copies:
         copy.wait_recv()
@@ -409,10 +478,12 @@
     def chosen(x):
         return jnp.where(core == 0, x, pltpu.roll(x, HD, 1))
 
-    here = jnp.concatenate([chosen(fhr0[...].astype(F32))[0:HALF], chosen(fin[0 : NT - HALF, :])], axis=0)
-    there = jnp.concatenate(
-        [chosen(fhr1[...].astype(F32))[0:HALF], chosen(frecv[...].astype(F32))[0 : NT - HALF]], axis=0
-    )
+    def opened(half):
+        half = half[...].astype(F32)[0:40]
+        return jnp.concatenate([half, pltpu.roll(half, HD, 1)], axis=0)[0:HALF]
+
+    here = jnp.concatenate([opened(fhr0), chosen(fin[0 : NT - HALF, :])], axis=0)
+    there = jnp.concatenate([opened(fhr1), chosen(frecv[...].astype(F32))[0 : NT - HALF]], axis=0)
     out[0:NT, :] = jnp.where(
         low, jnp.where(core == 0, here, there), pltpu.roll(jnp.where(core == 0, there, here), HD, 1)
     )
@@ -425,7 +496,7 @@
     total = za_own[z]
     for k in range(ZL - 1):
         total = total + za_recv[k].astype(F32)
-    out[NT + HD : NT + HD + 96, :] = total
+    out[NT + HD : NT + HD + 80, :] = total
 
     for copy in started:
         copy.wait_send()
@@ -443,7 +514,8 @@
     out_proj[...] = pltpu.roll(key_proj, HD, 1)[:, 0:HD]
     at = NT + 2 * HD
     out_bias[:, 0, 0:128] = parts[at : at + 9, :]
-    out_bias[:, 0, 128:144] = parts[at + 16 : at + 25, 0:16]
+    out_bias[0:7, 0, 128:144] = parts[at + 9 : at + 16, 0:16]
+    out_bias[7:9, 0, 128:144] = parts[at + 9 : at + 11, 16:32]
 
 
 def per_device(activations, qkv_weight, proj_weight, pos_bias, out_grad):
@@ -475,35 +547,43 @@
         v((CHIPS, 128, 128), F32),
         v((CHIPS, 128, 128), BF),
         v((CHIPS, 128, 128), BF),
-        v((CHIPS, 128, 128), F32),
-        v((CHIPS, 128, 128), BF),
-        v((CHIPS, 128, 128), BF),
+        v((CHIPS, HD, 128), F32),
+        v((CHIPS, HD, 128), BF),
+        v((CHIPS, HD, 128), BF),
+        v((CHIPS, HD, 128), F32),
+        v((CHIPS, HD, 128), BF),
+        v((CHIPS, HD, 128), BF),
         v((2, WT, WT), F32),
         v((WT, 256), BF),
         v((WT, 256), BF),
         v((4, 128, 128), BF),
         v((4, 128, 128), BF),
-        v((HPAD, 256), BF),
-        v((HPAD, 256), BF),
-        v((ZL, 96, 128), F32),
-        v((ZL, 96, 128), BF),
-        v((ZL - 1, 96, 128), BF),
-        v((ZL, 2, HD, 128), F32),
-        v((ZL, 2, HD, 128), BF),
-        v((ZL - 1, 2, HD, 128), BF),
+        v((96, 128), BF),
+        v((96, 128), BF),
+        v((ZL, 80, 128), F32),
+        v((ZL, 80, 128), BF),
+        v((ZL - 1, 80, 128), BF),
+        v((ZL, HD, 128), F32),
+        v((ZL, HD, 128), BF),
+        v((ZL - 1, HD, 128), BF),
+        v((ZL, HD, 128), F32),
+        v((ZL, HD, 128), BF),
+        v((ZL - 1, HD, 128), BF),
         v((HD, 128), BF),
         v((HD, 128), BF),
-        v((2, CHIPS, WT, 128), BF),
-        v((2, CHIPS - 1, WT, 128), BF),
+        v((2, 4, 2, WT, 128), BF),
+        v((2, 3, 2, WT, 128), BF),
+        v((2, WT, 128), BF),
+        v((2, WT, 128), BF),
         v((NT, 128), F32),
         v((NT, 128), BF),
         v((WT + HPAD, 128), BF),
-        v((HPAD, 128), BF),
-        v((HPAD, 128), BF),
-        v((HPAD, 128), BF),
+        v((2, 48, 128), BF),
+        v((48, 128), BF),
+        v((48, 128), BF),
         pltpu.SemaphoreType.DMA((5,)),
-        pltpu.SemaphoreType.DMA((64,)),
-        pltpu.SemaphoreType.DMA((64,)),
+        pltpu.SemaphoreType.DMA((72,)),
+        pltpu.SemaphoreType.DMA((72,)),
     ]
     hbm = pl.BlockSpec(memory_space=pl.ANY)
     vmem = pl.BlockSpec(memory_space=pltpu.VMEM)
@@ -515,7 +595,7 @@
     )
     parts = pl.pallas_call(
         kernel,
-        out_shape=jax.ShapeDtypeStruct((NT + HD + 96, 128), F32),
+        out_shape=jax.ShapeDtypeStruct((NT + HD + 80, 128), F32),
         in_specs=[hbm] * 5,
         out_specs=vmem,
         scratch_shapes=scratch,

time: 47.2 us -> 44.2 us (0.936)
  Pallas kernels: 46.4 us -> 43.4 us
    pallas_call x1, Pallas kernels: 44.5 us -> 41.5 us  [per_device(): pl.pallas_call(kernel, out_shape=jax.ShapeDtypeStruct((NT + HD + 80, 128)...]
where the time goes in v3:
time: 44.2 us; the launch traced here: 44.1 us
  Pallas kernels  43.4 us (98%)
  between operations  0.64 us (1%)
    pallas_call x1, Pallas kernels, per_device(): pl.pallas_call(kernel, out_shape=jax.ShapeDtypeStruct((NT + HD + 80, 128)...  41.5 us
    pallas_call x1, Pallas kernels, per_device(): pl.pallas_call(unpack, out_shape=shapes, in_specs=[vmem], out_specs=(vmem...  1.89 us

profile of v3, /device:TPU:1, one launch (start us, length us, event | category | flops | bytes accessed | tf_op | source)
XLA Modules:
  0.0 44.1 jit_solution(4023898794809915571)
XLA Ops:
  0.6 41.5 %shard_map.84.parts = f32[432,128]{1,0:T(8,128)} custom-call(bf16[24,12,2,1024]{3,2,1,0:T(2,128)(2,1)} %bitcast.5, bf16[3,64,1024]{2,1,0:T(8,128)(2,1)} %bitcast.6, bf16[64,1024]{1,0:T(8,128)(2,1)} %pw.1, f32[1,144,144]{2,1,0:T(8,128)} %pb.1, bf16[24,12,2,64]{3,2,1,0:T(2,128)(2,1)} %bitcast.7), custom_call_target="tpu_custom_call" | custom-call | tf_op jit(solution)/shard_map/pallas_call | solution.py:596
  42.2 1.9 %shard_map.85 = (bf16[24,12,2,64]{3,2,1,0:T(2,128)(2,1)}, f32[3,64,64]{2,1,0:T(8,128)}, f32[64,64]{1,0:T(8,128)}, f32[9,1,144]{2,1,0:T(1,128)}) custom-call(f32[432,128]{1,0:T(8,128)} %shard_map.84.parts), custom_call_target="tpu_custom_call" | custom-call | tf_op jit(solution)/shard_map/pallas_call | solution.py:612

commit v4 on v3

--- a/solution.py
+++ b/solution.py
@@ -55,6 +55,7 @@
     psend,
     precv,
     tsh,
+    town,
     tsend,
     trecv,
     w2,
@@ -99,9 +100,11 @@
     fin,
     fsend,
     frecv,
-    fhs,
-    fhr0,
-    fhr1,
+    hr_recv,
+    up_send,
+    up_recv,
+    fh_send,
+    fh_recv,
     lsem,
     ssem,
     rsem,
@@ -118,17 +121,18 @@
     sib = {"tp": sib_tp}
     down_same = {"lon": down}
     up_same = {"lon": up}
-    up_cross = {"lon": up, "tp": sib_tp}
-    down_cross = {"lon": down, "tp": sib_tp}
     across = {"lon": (1 - xh) * ZL + z}
     chips = [None] + [{"tp": lax.rem(chip + k, CHIPS) * 2 + core} for k in range(1, CHIPS)]
     row, side = lax.div(chip, 2), lax.rem(chip, 2)
     ys = [None] + [{"tp": (lax.rem(row + k, 4) * 2 + side) * 2 + core} for k in range(1, 4)]
-    beside = {"tp": (row * 2 + 1 - side) * 2 + core}
+    beside_tp = (row * 2 + 1 - side) * 2 + core
+    beside = {"tp": beside_tp}
+    up_beside = {"lon": up, "tp": beside_tp}
+    down_beside = {"lon": down, "tp": beside_tp}
     zs = [None] + [{"lon": xh * ZL + lax.rem(z + k, ZL)} for k in range(1, ZL)]
 
     barrier = pltpu.get_barrier_semaphore()
-    peers = [sib] + chips[1:] + [down_same, up_same, up_cross, down_cross, across] + zs[1:]
+    peers = [sib] + chips[1:] + [down_same, up_same, up_beside, down_beside, across] + zs[1:]
     for peer in peers:
         pl.semaphore_signal(barrier, inc=1, device_id=peer, device_id_type=MESH)
 
@@ -195,6 +199,7 @@
     p_copy.wait_recv()
     mine = low == (core == 0)
     merged = jnp.where(mine, pf[...], pltpu.roll(precv[...].astype(F32), HD, 1))
+    town[...] = merged[0:HPAD]
     tsend[...] = merged[0:HPAD].astype(BF)
     t_copy = go(remote(tsend, trecv, down_same))
     tsh[0 : NT - HALF, :] = merged[HALF:NT]
@@ -281,8 +286,9 @@
         dqkv_s[r, 128:256] = jnp.where(low, dk[0], dk[1]).astype(BF)
         dqkv_s[r, 256:384] = jnp.where(low, dv[0], dv[1]).astype(BF)
 
-    early, late, halo, rest = (0, 0, 80), (0, 80, 64), (1, 64, 80), (1, 0, 64)
+    early, late, rest = (0, 0, 80), (0, 80, 64), (1, 0, 80)
     rs = {}
+    over = pl.ds(WT - HPAD, HPAD)
 
     def send_out(part):
         w, a, n = part
@@ -333,7 +339,10 @@
     backward(1)
 
     input_grad(1)
-    send_out(halo)
+    halo_copies = []
+    for k in range(1, 4):
+        to = lax.rem(row + k, 4)
+        halo_copies.append(go(remote(rs_send.at[1, to, :, over], hr_recv.at[k - 1], ys[k])))
     b_send[:, 0:WT] = b_own[1].astype(BF)
     b_copy = go(remote(b_send, b_recv, sib))
     weight_grad((0, 2), ma_own, ma_send)
@@ -414,19 +423,18 @@
         fsend[r, :] = total.astype(BF)
 
     rx_late = pass_over(late)
-    rx_halo = pass_over(halo)
+    for copy in halo_copies:
+        copy.wait_recv()
+    for i, (which, peer) in enumerate([(side, up_same), (1 - side, up_beside)]):
+        total = rs_send[1, row, which, over].astype(F32)
+        for k in range(3):
+            total = total + hr_recv[k, which].astype(F32)
+        up_send[i] = total.astype(BF)
+    up_copies = [
+        go(remote(up_send.at[i], up_recv.at[i], peer)) for i, peer in enumerate((up_same, up_beside))
+    ]
     finish(late, rx_late)
-    finish(halo, rx_halo)
-    moved = jnp.concatenate([fin[NT - HALF : NT, :], jnp.zeros((HPAD - HALF, 128), F32)], axis=0)
-    turned = pltpu.roll(moved, HD, 1)
-    firsts = jnp.where(low, moved[0:40], turned[40:80])
-    seconds = jnp.where(low, turned[0:40], moved[40:80])
-    mine_half = jnp.where(core == 0, firsts, seconds)
-    other_half = jnp.where(core == 0, seconds, firsts)
-    blank = jnp.zeros((8, 128), F32)
-    fhs[0] = jnp.concatenate([mine_half, blank], axis=0).astype(BF)
-    fhs[1] = jnp.concatenate([other_half, blank], axis=0).astype(BF)
-    f_copies = [go(remote(fhs.at[0], fhr0, up_same)), go(remote(fhs.at[1], fhr1, up_cross))]
+    f_copies = []
 
     ma_copies[1].wait_recv()
     xa_copy.wait_recv()
@@ -451,6 +459,12 @@
 
     rx_early = pass_over(early)
     rx_rest = pass_over(rest)
+    for copy in up_copies:
+        copy.wait_recv()
+    moved = up_recv[0].astype(F32) + up_recv[1].astype(F32)
+    moved = moved[HPAD - HALF : HPAD] + town[0:HALF]
+    fh_send[...] = jnp.concatenate([moved, jnp.zeros((HPAD - HALF, 128), F32)], axis=0).astype(BF)
+    f_copies.append(go(remote(fh_send, fh_recv, sib)))
     finish(early, rx_early)
     f_copies.append(go(remote(fsend.at[0:WT], frecv.at[0:WT], sib)))
     finish(rest, rx_rest)
@@ -478,12 +492,9 @@
     def chosen(x):
         return jnp.where(core == 0, x, pltpu.roll(x, HD, 1))
 
-    def opened(half):
-        half = half[...].astype(F32)[0:40]
-        return jnp.concatenate([half, pltpu.roll(half, HD, 1)], axis=0)[0:HALF]
-
-    here = jnp.concatenate([opened(fhr0), chosen(fin[0 : NT - HALF, :])], axis=0)
-    there = jnp.concatenate([opened(fhr1), chosen(frecv[...].astype(F32))[0 : NT - HALF]], axis=0)
+    here = chosen(jnp.concatenate([moved, fin[0 : NT - HALF, :]], axis=0))
+    there = jnp.concatenate([fh_recv[...].astype(F32)[0:HALF], frecv[...].astype(F32)[0 : NT - HALF]], axis=0)
+    there = chosen(there)
     out[0:NT, :] = jnp.where(
         low, jnp.where(core == 0, here, there), pltpu.roll(jnp.where(core == 0, there, here), HD, 1)
     )
@@ -534,6 +545,7 @@
         v((NT, 128), BF),
         v((NT, 128), BF),
         v((NT, 128), F32),
+        v((HPAD, 128), F32),
         v((HPAD, 128), BF),
         v((HPAD, 128), BF),
         v((3, 2, HD, D), BF),
@@ -578,9 +590,11 @@
         v((NT, 128), F32),
         v((NT, 128), BF),
         v((WT + HPAD, 128), BF),
-        v((2, 48, 128), BF),
-        v((48, 128), BF),
-        v((48, 128), BF),
+        v((3, 2, HPAD, 128), BF),
+        v((2, HPAD, 128), BF),
+        v((2, HPAD, 128), BF),
+        v((HPAD, 128), BF),
+        v((HPAD, 128), BF),
         pltpu.SemaphoreType.DMA((5,)),
         pltpu.SemaphoreType.DMA((72,)),
         pltpu.SemaphoreType.DMA((72,)),

time: 44.2 us -> 42.9 us (0.971)
  Pallas kernels: 43.4 us -> 41.8 us
    pallas_call x1, Pallas kernels: 41.5 us -> 39.9 us  [per_device(): pl.pallas_call(kernel, out_shape=jax.ShapeDtypeStruct((NT + HD + 80, 128)...]
where the time goes in v4:
time: 42.9 us; the launch traced here: 42.4 us
  Pallas kernels  41.8 us (97%)
  between operations  0.64 us (1%)
    pallas_call x1, Pallas kernels, per_device(): pl.pallas_call(kernel, out_shape=jax.ShapeDtypeStruct((NT + HD + 80, 128)...  39.9 us
    pallas_call x1, Pallas kernels, per_device(): pl.pallas_call(unpack, out_shape=shapes, in_specs=[vmem], out_specs=(vmem...  1.89 us

profile of v4, /device:TPU:1, one launch (start us, length us, event | category | flops | bytes accessed | tf_op | source)
XLA Modules:
  0.0 42.4 jit_solution(9122078350961372773)
XLA Ops:
  0.6 39.9 %shard_map.84.parts = f32[432,128]{1,0:T(8,128)} custom-call(bf16[24,12,2,1024]{3,2,1,0:T(2,128)(2,1)} %bitcast.5, bf16[3,64,1024]{2,1,0:T(8,128)(2,1)} %bitcast.6, bf16[64,1024]{1,0:T(8,128)(2,1)} %pw.1, f32[1,144,144]{2,1,0:T(8,128)} %pb.1, bf16[24,12,2,64]{3,2,1,0:T(2,128)(2,1)} %bitcast.7), custom_call_target="tpu_custom_call" | custom-call | tf_op jit(solution)/shard_map/pallas_call | solution.py:610
  40.5 1.9 %shard_map.85 = (bf16[24,12,2,64]{3,2,1,0:T(2,128)(2,1)}, f32[3,64,64]{2,1,0:T(8,128)}, f32[64,64]{1,0:T(8,128)}, f32[9,1,144]{2,1,0:T(1,128)}) custom-call(f32[432,128]{1,0:T(8,128)} %shard_map.84.parts), custom_call_target="tpu_custom_call" | custom-call | tf_op jit(solution)/shard_map/pallas_call | solution.py:626

commit v5 on v4

--- a/solution.py
+++ b/solution.py
@@ -194,7 +194,9 @@
         hs[CELLS * l : CELLS * (l + 1), :] = row_of(l)
     hs[HALF:HPAD, :] = jnp.zeros((HPAD - HALF, D), F32)
     hsend[...] = hs[...].astype(BF)
-    h_copy = go(remote(hsend, hrecv, down_same))
+    plain = lax.div(z + ZL - 1, ZL)
+    h_peer = {"lon": down, "tp": beside_tp + (tp - beside_tp) * plain}
+    h_copy = go(remote(hsend, hrecv, h_peer))
 
     p_copy.wait_recv()
     mine = low == (core == 0)
@@ -258,10 +260,6 @@
 
     forward(0)
 
-    h_copy.wait_recv()
-    xs[NT - HALF : NT, :] = hrecv[...].astype(F32)[0:HALF]
-    norm(1)
-    forward(1)
 
     def backward(w):
         r = pl.ds(WT * w, WT)
@@ -317,6 +315,11 @@
         copy.wait_recv()
     backward(0)
     input_grad(0)
+
+    h_copy.wait_recv()
+    xs[NT - HALF : NT, :] = hrecv[...].astype(F32)[0:HALF]
+    norm(1)
+    forward(1)
 
     for copy in ag[1]:
         copy.wait_recv()

time: 42.9 us -> 42.1 us (0.981)
  Pallas kernels: 41.8 us -> 41.2 us
    pallas_call x1, Pallas kernels: 39.9 us -> 39.3 us  [per_device(): pl.pallas_call(kernel, out_shape=jax.ShapeDtypeStruct((NT + HD + 80, 128)...]
where the time goes in v5:
time: 42.1 us; the launch traced here: 41.8 us
  Pallas kernels  41.2 us (98%)
  between operations  0.64 us (2%)
    pallas_call x1, Pallas kernels, per_device(): pl.pallas_call(kernel, out_shape=jax.ShapeDtypeStruct((NT + HD + 80, 128)...  39.3 us
    pallas_call x1, Pallas kernels, per_device(): pl.pallas_call(unpack, out_shape=shapes, in_specs=[vmem], out_specs=(vmem...  1.89 us

profile of v5, /device:TPU:1, one launch (start us, length us, event | category | flops | bytes accessed | tf_op | source)
XLA Modules:
  0.0 41.8 jit_solution(12402229790621085082)
XLA Ops:
  0.6 39.3 %shard_map.84.parts = f32[432,128]{1,0:T(8,128)} custom-call(bf16[24,12,2,1024]{3,2,1,0:T(2,128)(2,1)} %bitcast.5, bf16[3,64,1024]{2,1,0:T(8,128)(2,1)} %bitcast.6, bf16[64,1024]{1,0:T(8,128)(2,1)} %pw.1, f32[1,144,144]{2,1,0:T(8,128)} %pb.1, bf16[24,12,2,64]{3,2,1,0:T(2,128)(2,1)} %bitcast.7), custom_call_target="tpu_custom_call" | custom-call | tf_op jit(solution)/shard_map/pallas_call | solution.py:613
  39.9 1.9 %shard_map.85 = (bf16[24,12,2,64]{3,2,1,0:T(2,128)(2,1)}, f32[3,64,64]{2,1,0:T(8,128)}, f32[64,64]{1,0:T(8,128)}, f32[9,1,144]{2,1,0:T(1,128)}) custom-call(f32[432,128]{1,0:T(8,128)} %shard_map.84.parts), custom_call_target="tpu_custom_call" | custom-call | tf_op jit(solution)/shard_map/pallas_call | solution.py:629

commit v6 on v5

--- a/solution.py
+++ b/solution.py
@@ -42,6 +42,7 @@
     pb,
     og,
     out,
+    outv,
     act_v,
     og_v,
     xs,
@@ -56,7 +57,6 @@
     precv,
     tsh,
     town,
-    tsend,
     trecv,
     w2,
     pw2,
@@ -129,10 +129,13 @@
     beside = {"tp": beside_tp}
     up_beside = {"lon": up, "tp": beside_tp}
     down_beside = {"lon": down, "tp": beside_tp}
+    up_cross = {"lon": up, "tp": sib_tp}
+    down_cross = {"lon": down, "tp": sib_tp}
     zs = [None] + [{"lon": xh * ZL + lax.rem(z + k, ZL)} for k in range(1, ZL)]
 
     barrier = pltpu.get_barrier_semaphore()
-    peers = [sib] + chips[1:] + [down_same, up_same, up_beside, down_beside, across] + zs[1:]
+    peers = [down_same, up_same, up_beside, down_beside, up_cross, down_cross, across]
+    peers = peers + zs[4:] + zs[1:4] + chips[1:] + [sib]
     for peer in peers:
         pl.semaphore_signal(barrier, inc=1, device_id=peer, device_id_type=MESH)
 
@@ -178,6 +181,8 @@
     pl.semaphore_wait(barrier, len(peers))
 
     p_copy = go(remote(psend, precv, sib))
+    first = psend.at[0:HPAD]
+    t_copies = [go(remote(first, trecv.at[0], down_same)), go(remote(first, trecv.at[1], down_cross))]
     for load in loads[1:4]:
         load.wait()
     w_copy = go(remote(w2.at[:, 0], w2.at[:, 1], sib))
@@ -202,8 +207,6 @@
     mine = low == (core == 0)
     merged = jnp.where(mine, pf[...], pltpu.roll(precv[...].astype(F32), HD, 1))
     town[...] = merged[0:HPAD]
-    tsend[...] = merged[0:HPAD].astype(BF)
-    t_copy = go(remote(tsend, trecv, down_same))
     tsh[0 : NT - HALF, :] = merged[HALF:NT]
     g[0, chip] = merged[HALF : HALF + WT].astype(BF)
     ag = [[], []]
@@ -227,8 +230,12 @@
 
         lax.fori_loop(0, 3, body, 0)
 
-    t_copy.wait_recv()
-    tsh[NT - HALF : NT, :] = trecv[...].astype(F32)[0:HALF]
+    for copy in t_copies:
+        copy.wait_recv()
+    ahead_rows = jnp.where(
+        mine, trecv[0].astype(F32), pltpu.roll(trecv[1].astype(F32), HD, 1)
+    )
+    tsh[NT - HALF : NT, :] = ahead_rows[0:HALF]
     g[1, chip] = tsh[WT:NT, :].astype(BF)
     for k in range(1, CHIPS):
         ag[1].append(go(remote(g.at[1, chip], g.at[1, chip], chips[k])))
@@ -498,19 +505,26 @@
     here = chosen(jnp.concatenate([moved, fin[0 : NT - HALF, :]], axis=0))
     there = jnp.concatenate([fh_recv[...].astype(F32)[0:HALF], frecv[...].astype(F32)[0 : NT - HALF]], axis=0)
     there = chosen(there)
-    out[0:NT, :] = jnp.where(
+    outv[0:NT, :] = jnp.where(
         low, jnp.where(core == 0, here, there), pltpu.roll(jnp.where(core == 0, there, here), HD, 1)
     )
 
+    stores = [pltpu.make_async_copy(outv.at[0:NT], out.at[0:NT], lsem.at[0])]
+    stores[0].start()
     xb_copy.wait_recv()
-    out[NT : NT + HD, :] = second_half + xb_recv[...].astype(F32)
+    outv[NT : NT + HD, :] = second_half + xb_recv[...].astype(F32)
 
     for copy in za_copies:
         copy.wait_recv()
     total = za_own[z]
     for k in range(ZL - 1):
         total = total + za_recv[k].astype(F32)
-    out[NT + HD : NT + HD + 80, :] = total
+    outv[NT + HD : NT + HD + 80, :] = total
+    tail = pl.ds(NT, HD + 80)
+    stores.append(pltpu.make_async_copy(outv.at[tail], out.at[tail], lsem.at[1]))
+    stores[1].start()
+    for store in stores:
+        store.wait()
 
     for copy in started:
         copy.wait_send()
@@ -535,6 +549,7 @@
 def per_device(activations, qkv_weight, proj_weight, pos_bias, out_grad):
     v = pltpu.VMEM
     scratch = [
+        v((NT + HD + 80, 128), F32),
         v((LON, CELLS, ROWS, D), BF),
         v((LON, CELLS, ROWS, HD), BF),
         v((NT, D), F32),
@@ -549,8 +564,7 @@
         v((NT, 128), BF),
         v((NT, 128), F32),
         v((HPAD, 128), F32),
-        v((HPAD, 128), BF),
-        v((HPAD, 128), BF),
+        v((2, HPAD, 128), BF),
         v((3, 2, HD, D), BF),
         v((2, HD, D), BF),
         v((2, WT, WT), F32),
@@ -614,7 +628,7 @@
         kernel,
         out_shape=jax.ShapeDtypeStruct((NT + HD + 80, 128), F32),
         in_specs=[hbm] * 5,
-        out_specs=vmem,
+        out_specs=hbm,
         scratch_shapes=scratch,
         compiler_params=pltpu.CompilerParams(
             collective_id=0, has_side_effects=True, vmem_limit_bytes=60 << 20

time: 42.1 us -> 41.8 us (level)
  no operation moved by 1% of the time
where the time goes in v6:
time: 41.8 us; the launch traced here: 41.6 us
  Pallas kernels  41 us (98%)
  between operations  0.64 us (2%)
    pallas_call x1, Pallas kernels, per_device(): pl.pallas_call(kernel, out_shape=jax.ShapeDtypeStruct((NT + HD + 80, 128)...  39.1 us
    pallas_call x1, Pallas kernels, per_device(): pl.pallas_call(unpack, out_shape=shapes, in_specs=[vmem], out_specs=(vmem...  1.89 us

profile of v6, /device:TPU:1, one launch (start us, length us, event | category | flops | bytes accessed | tf_op | source)
XLA Modules:
  0.0 41.6 jit_solution(2415691003021458273)
XLA Ops:
  0.6 39.1 %shard_map.84.parts = f32[432,128]{1,0:T(8,128)} custom-call(bf16[24,12,2,1024]{3,2,1,0:T(2,128)(2,1)} %bitcast.5, bf16[3,64,1024]{2,1,0:T(8,128)(2,1)} %bitcast.6, bf16[64,1024]{1,0:T(8,128)(2,1)} %pw.1, f32[1,144,144]{2,1,0:T(8,128)} %pb.1, bf16[24,12,2,64]{3,2,1,0:T(2,128)(2,1)} %bitcast.7), custom_call_target="tpu_custom_call" | custom-call | tf_op jit(solution)/shard_map/pallas_call | solution.py:627
  39.7 1.9 %shard_map.85 = (bf16[24,12,2,64]{3,2,1,0:T(2,128)(2,1)}, f32[3,64,64]{2,1,0:T(8,128)}, f32[64,64]{1,0:T(8,128)}, f32[9,1,144]{2,1,0:T(1,128)}) custom-call(f32[432,128]{1,0:T(8,128)} %shard_map.84.parts), custom_call_target="tpu_custom_call" | custom-call | tf_op jit(solution)/shard_map/pallas_call | solution.py:643

commit v7 on v6

--- a/solution.py
+++ b/solution.py
@@ -389,12 +389,12 @@
     zp_copies = start_z(mp_copy, mp_own, mp_recv, zp_own, zp_send, zp_recv)
     weight_grad((1,), mk_own, mk_send)
     mk_copy = go(remote(mk_send, mk_recv, sib))
-    send_out(early)
-    send_out(rest)
 
     ma_copies[0].wait_recv()
     for j in range(4):
         xa_send[j] = (ma_own[far + j] + ma_recv[far + j].astype(F32)).astype(BF)
+    send_out(early)
+    send_out(rest)
     xa_copy = go(remote(xa_send, xa_recv, across))
     zk_copies = start_z(mk_copy, mk_own, mk_recv, zk_own, zk_send, zk_recv)
     b_copy.wait_recv()

time: 41.8 us -> 41.7 us (level)
  no operation moved by 1% of the time
where the time goes in v7:
time: 41.7 us; the launch traced here: 41.6 us
  Pallas kernels  40.9 us (98%)
  between operations  0.64 us (2%)
    pallas_call x1, Pallas kernels, per_device(): pl.pallas_call(kernel, out_shape=jax.ShapeDtypeStruct((NT + HD + 80, 128)...  39 us
    pallas_call x1, Pallas kernels, per_device(): pl.pallas_call(unpack, out_shape=shapes, in_specs=[vmem], out_specs=(vmem...  1.89 us

profile of v7, /device:TPU:1, one launch (start us, length us, event | category | flops | bytes accessed | tf_op | source)
XLA Modules:
  0.0 41.6 jit_solution(14543304597564399024)
XLA Ops:
  0.6 39.0 %shard_map.84.parts = f32[432,128]{1,0:T(8,128)} custom-call(bf16[24,12,2,1024]{3,2,1,0:T(2,128)(2,1)} %bitcast.5, bf16[3,64,1024]{2,1,0:T(8,128)(2,1)} %bitcast.6, bf16[64,1024]{1,0:T(8,128)(2,1)} %pw.1, f32[1,144,144]{2,1,0:T(8,128)} %pb.1, bf16[24,12,2,64]{3,2,1,0:T(2,128)(2,1)} %bitcast.7), custom_call_target="tpu_custom_call" | custom-call | tf_op jit(solution)/shard_map/pallas_call | solution.py:627
  39.7 1.9 %shard_map.85 = (bf16[24,12,2,64]{3,2,1,0:T(2,128)(2,1)}, f32[3,64,64]{2,1,0:T(8,128)}, f32[64,64]{1,0:T(8,128)}, f32[9,1,144]{2,1,0:T(1,128)}) custom-call(f32[432,128]{1,0:T(8,128)} %shard_map.84.parts), custom_call_target="tpu_custom_call" | custom-call | tf_op jit(solution)/shard_map/pallas_call | solution.py:643
